TPU v7x, 32 devices: a whole 2x2x4 slice. The times are simulated.
32 devices in a mesh: dp: 2 (over x), outer: 8 (over z, y), inner: 2 (over core).
Axes of the slice: x: 2, y: 2, z: 4, core: 2. Of those that a mesh axis runs over, the one named last changes fastest.
Arguments:
- tokens: bfloat16 [1024, 4096], P(('dp', 'outer', 'inner')), may hold values from -6 to 6
- expert_ids: int32 [1024, 8], P(('dp', 'outer', 'inner')), may hold values from 0 to 15, all different within a row; in each aligned block of 32 rows (0 to 31, 32 to 63, ...) at most 24 rows name the same one
- gate_values: float32 [1024, 8], P(('dp', 'outer', 'inner')), may hold values from 0.02 to 0.5
- upstream: bfloat16 [1024, 4096], P(('dp', 'outer', 'inner')), may hold values from -1.5 to 1.5
- w_gate: bfloat16 [16, 4096, 768], P(('outer', 'inner')), may hold values from -0.09375 to 0.09375
- w_up: bfloat16 [16, 4096, 768], P(('outer', 'inner')), may hold values from -0.09375 to 0.09375
- w_down: bfloat16 [16, 768, 4096], P(('outer', 'inner')), may hold values from -0.21875 to 0.21875
Outputs:
- output: bfloat16 [1024, 4096], P(('dp', 'outer', 'inner'))
- grad_tokens: bfloat16 [1024, 4096], P(('dp', 'outer', 'inner'))
- grad_gates: float32 [1024, 8], P(('dp', 'outer', 'inner'))
- grad_w_gate: bfloat16 [16, 4096, 768], P(('outer', 'inner'), 'dp')
- grad_w_up: bfloat16 [16, 4096, 768], P(('outer', 'inner'), 'dp')
- grad_w_down: bfloat16 [16, 768, 4096], P(('outer', 'inner'), None, 'dp')
Inputs may be any that keep to these rules, and one draw needn't show every extreme that they name: `expert_ids`: each token names 8 different experts. Among the 32 tokens of one device (aligned blocks of rows), no expert is named more than 24 times, a bound that some block reaches.
All inputs are finite; a program needn't handle non-finite values.
Results may differ from a plain program's by a relative error of at most 0.013.
Values may be sent and summed in bfloat16 or wider, within the bound.
A program may use at most 192 MiB of HBM per device.

v0:
```python
import jax
import jax.numpy as jnp
from jax import lax
from jax.sharding import PartitionSpec as P


def contract_last(left, right):
    return lax.dot_general(
        left, right, (((1,), (1,)), ((), ())), preferred_element_type=jnp.float32
    )


def contract_first(left, right):
    return lax.dot_general(
        left, right, (((0,), (0,)), ((), ())), preferred_element_type=jnp.float32
    )


def expert_rows(rows_in, grads_in, gate_mat, up_mat, down_mat):
    gate_pre = jnp.dot(rows_in, gate_mat, preferred_element_type=jnp.float32)
    up_pre = jnp.dot(rows_in, up_mat, preferred_element_type=jnp.float32)
    sigma = jax.nn.sigmoid(gate_pre)
    silu_value = gate_pre * sigma
    hidden = (silu_value * up_pre).astype(jnp.bfloat16)
    expert_out = jnp.dot(hidden, down_mat, preferred_element_type=jnp.float32).astype(jnp.bfloat16)
    grad_hidden = contract_last(grads_in, down_mat)
    slope = sigma * (1.0 + gate_pre * (1.0 - sigma))
    grad_gate_pre = (grad_hidden * up_pre * slope).astype(jnp.bfloat16)
    grad_up_pre = (grad_hidden * silu_value).astype(jnp.bfloat16)
    pair_grad = (
        contract_last(grad_gate_pre, gate_mat) + contract_last(grad_up_pre, up_mat)
    ).astype(jnp.bfloat16)
    return (hidden, expert_out, grad_gate_pre, grad_up_pre, pair_grad)


def local(tokens, expert_ids, gate_values, upstream, w_gate, w_up, w_down):
    local_tokens = tokens.shape[0]
    width = tokens.shape[1]
    top_count = expert_ids.shape[1]
    ff_width = w_gate.shape[2]
    outer_count = lax.axis_size("outer")
    inner_count = lax.axis_size("inner")
    expert_count = outer_count * inner_count
    capacity = min(local_tokens, 3 * local_tokens * top_count // (2 * expert_count))
    pair_count = local_tokens * top_count
    flat_ids = expert_ids.reshape(-1)
    flat_gates = gate_values.reshape(-1)
    onehot = (flat_ids[:, None] == jnp.arange(expert_count, dtype=jnp.int32)[None, :]).astype(
        jnp.int32
    )
    slot_rank = jnp.sum((jnp.cumsum(onehot, axis=0) - onehot) * onehot, axis=1)
    pair_slot = flat_ids * capacity + slot_rank
    slot_pair = (
        jnp.full((expert_count * capacity,), pair_count, jnp.int32)
        .at[pair_slot]
        .set(jnp.arange(pair_count, dtype=jnp.int32))
    )
    slot_token = jnp.where(slot_pair < pair_count, slot_pair // top_count, local_tokens)
    token_pad = jnp.concatenate([tokens, jnp.zeros((1, width), jnp.bfloat16)], axis=0)
    upstream_pad = jnp.concatenate([upstream, jnp.zeros((1, width), jnp.bfloat16)], axis=0)
    gate_pad = jnp.concatenate([flat_gates, jnp.zeros((1,), jnp.float32)], axis=0)
    send_rows = token_pad[slot_token]
    send_grads = (
        gate_pad[slot_pair][:, None] * upstream_pad[slot_token].astype(jnp.float32)
    ).astype(jnp.bfloat16)
    flat_shape = (expert_count, capacity, width)
    got_rows, got_grads = (
        lax.all_to_all(
            send_rows.reshape(flat_shape),
            ("outer", "inner"),
            split_axis=0,
            concat_axis=0,
            tiled=True,
        ),
        lax.all_to_all(
            send_grads.reshape(flat_shape),
            ("outer", "inner"),
            split_axis=0,
            concat_axis=0,
            tiled=True,
        ),
    )
    rows_in = got_rows.reshape(-1, width)
    grads_in = got_grads.reshape(-1, width)
    hidden, expert_out, grad_gate_pre, grad_up_pre, pair_grad = expert_rows(
        rows_in, grads_in, w_gate[0], w_up[0], w_down[0]
    )
    back_out, back_grad = (
        lax.all_to_all(
            expert_out.reshape(flat_shape),
            ("outer", "inner"),
            split_axis=0,
            concat_axis=0,
            tiled=True,
        ),
        lax.all_to_all(
            pair_grad.reshape(flat_shape),
            ("outer", "inner"),
            split_axis=0,
            concat_axis=0,
            tiled=True,
        ),
    )
    joined_grads = jnp.concatenate([grad_gate_pre, grad_up_pre], axis=1)
    columns = rows_in
    grad_joined = lax.psum_scatter(
        contract_first(columns, joined_grads).astype(jnp.bfloat16),
        "dp",
        scatter_dimension=0,
        tiled=True,
    ).astype(jnp.float32)
    columns = grads_in
    grad_down = (
        lax.psum_scatter(
            contract_first(columns, hidden).astype(jnp.bfloat16),
            "dp",
            scatter_dimension=0,
            tiled=True,
        )
        .astype(jnp.float32)
        .T
    )
    pair_out = back_out.reshape(-1, width)[pair_slot].reshape(local_tokens, top_count, width)
    pair_back = back_grad.reshape(-1, width)[pair_slot].reshape(local_tokens, top_count, width)
    output = jnp.sum(gate_values[:, :, None] * pair_out.astype(jnp.float32), axis=1).astype(
        jnp.bfloat16
    )
    grad_tokens = jnp.sum(pair_back.astype(jnp.float32), axis=1).astype(jnp.bfloat16)
    grad_gates = jnp.einsum("tkd,td->tk", pair_out, upstream, preferred_element_type=jnp.float32)
    grad_w_gate = grad_joined[:, :ff_width].astype(jnp.bfloat16)[None]
    grad_w_up = grad_joined[:, ff_width:].astype(jnp.bfloat16)[None]
    grad_w_down = grad_down.astype(jnp.bfloat16)[None]
    return (output, grad_tokens, grad_gates, grad_w_gate, grad_w_up, grad_w_down)


def solution(mesh):
    placed = (
        P(("dp", "outer", "inner"), None),
        P(("dp", "outer", "inner"), None),
        P(("dp", "outer", "inner"), None),
        P(("dp", "outer", "inner"), None),
        P(("outer", "inner"), None, None),
        P(("outer", "inner"), None, None),
        P(("outer", "inner"), None, None),
    )
    return jax.shard_map(
        local,
        mesh=mesh,
        in_specs=placed,
        out_specs=(
            P(("dp", "outer", "inner"), None),
            P(("dp", "outer", "inner"), None),
            P(("dp", "outer", "inner"), None),
            P(("outer", "inner"), "dp", None),
            P(("outer", "inner"), "dp", None),
            P(("outer", "inner"), None, "dp"),
        ),
        check_vma=False,
    )
```

profile of v0, /device:TPU:0, one launch (start us, length us, event | category | flops | bytes accessed | tf_op | source)
XLA Modules:
  0.0 431.7 jit_solution(3533371723951586610)
XLA Ops:
  16.1 3.3 gather_fusion.3
  22.1 7.4 %all-to-all-start.2 = ((bf16[16,24,4096]{2,1,0:T(8,128)(2,1)}), bf16[16,24,4096]{2,1,0:T(8,128)(2,1)S(1)}, u32[]{:S(2)}, u32[]{:S(2)}) async-start(bf16[16,24,4096]{2,1,0:T(8,128)(2,1)} %fusion), calls=%async_computation.2 | async-start | bytes 6291456 | tf_op jit(solution)/shard_map/all_to_all | solution.py:75
  30.4 4.0 gather_fusion
  34.5 54.4 %all-to-all-done.2 = bf16[16,24,4096]{2,1,0:T(8,128)(2,1)S(1)} async-done(((bf16[16,24,4096]{2,1,0:T(8,128)(2,1)}), bf16[16,24,4096]{2,1,0:T(8,128)(2,1)S(1)}, u32[]{:S(2)}, u32[]{:S(2)}) %all-to-all-start.2) | async-done | bytes 3145760 | tf_op jit(solution)/shard_map/all_to_all | solution.py:75
  88.8 15.5 %all-to-all-start = ((bf16[16,24,4096]{2,1,0:T(8,128)(2,1)}), bf16[16,24,4096]{2,1,0:T(8,128)(2,1)}, u32[]{:S(2)}, u32[]{:S(2)}) async-start(bf16[16,24,4096]{2,1,0:T(8,128)(2,1)} %bitcast.3), calls=%async_computation | async-start | bytes 6291456 | tf_op jit(solution)/shard_map/all_to_all | solution.py:68
  104.5 6.4 %fusion.1 = f32[384,768]{1,0:T(8,128)} fusion(bf16[384,4096]{1,0:T(8,128)(2,1)S(1)} %bitcast.79, bf16[1,768,4096]{2,1,0:T(8,128)(2,1)} %param.13), kind=kOutput, calls=%fused_computation.10 | convolution fusion | flops 2415919104 | bytes 10616832 | tf_op jit(solution)/shard_map/dot_general | solution.py:8
  111.0 52.8 %all-to-all-done = bf16[16,24,4096]{2,1,0:T(8,128)(2,1)} async-done(((bf16[16,24,4096]{2,1,0:T(8,128)(2,1)}), bf16[16,24,4096]{2,1,0:T(8,128)(2,1)}, u32[]{:S(2)}, u32[]{:S(2)}) %all-to-all-start) | async-done | bytes 3145760 | tf_op jit(solution)/shard_map/all_to_all | solution.py:68
  163.7 6.4 %fusion.7 = f32[384,768]{1,0:T(8,128)S(1)} fusion(bf16[384,4096]{1,0:T(8,128)(2,1)} %bitcast.4, bf16[1,4096,768]{2,1,0:T(8,128)(2,1)} %param.12), kind=kOutput, calls=%fused_computation.16 | convolution fusion | flops 2415919104 | bytes 10616832 | tf_op jit(solution)/shard_map/dot_general | solution.py:21
  170.2 7.7 %multiply_convert_fusion.1 = (bf16[384,768]{1,0:T(8,128)(2,1)}, bf16[384,768]{1,0:T(8,128)(2,1)}, bf16[384,768]{1,0:T(8,128)(2,1)S(1)}) fusion(f32[384,768]{1,0:T(8,128)S(1)} %copy-done.7, f32[384,768]{1,0:T(8,128)S(1)} %fusion.7, bf16[384,4096]{1,0:T(8,128)(2,1)} %bitcast.4, bf16[1,4096,768]{2,1,0:T(8,128)(2,1)} %param.11), kind=kOutput, calls=%fused_computation.34 | convolution fusion | flops 2420342784 | bytes 13565952 | tf_op jit(solution)/shard_map/dot_general | solution.py:20
  178.7 5.4 %convolution_convert_fusion.1 = bf16[4096,768]{1,0:T(8,128)(2,1)} fusion(bf16[384,4096]{1,0:T(8,128)(2,1)S(1)} %bitcast.80, bf16[384,768]{1,0:T(8,128)(2,1)S(1)} %get-tuple-element.22), kind=kOutput, calls=%fused_computation.7 | convolution fusion | flops 2419064832 | bytes 10027008 | tf_op jit(solution)/shard_map/dot_general | solution.py:14
  185.3 11.6 %convolution_convert_fusion = bf16[4096,1536]{1,0:T(8,128)(2,1)} fusion(bf16[384,4096]{1,0:T(8,128)(2,1)} %bitcast.4, bf16[384,768]{1,0:T(8,128)(2,1)S(1)} %copy-done.2, bf16[384,768]{1,0:T(8,128)(2,1)S(1)} %copy-done.5), kind=kOutput, calls=%fused_computation.6 | convolution fusion | flops 4840488960 | bytes 16908288 | tf_op jit(solution)/shard_map/dot_general | solution.py:14
  198.0 6.7 %fusion.15 = bf16[384,4096]{1,0:T(8,128)(2,1)} fusion(bf16[384,768]{1,0:T(8,128)(2,1)S(1)} %copy-done.4, bf16[1,768,4096]{2,1,0:T(8,128)(2,1)} %param.13), kind=kOutput, calls=%fused_computation.23 | convolution fusion | flops 2417491968 | bytes 10027008 | tf_op jit(solution)/shard_map/dot_general | solution.py:25
  204.8 15.4 %all-to-all-start.1 = ((bf16[16,24,4096]{2,1,0:T(8,128)(2,1)}), bf16[16,24,4096]{2,1,0:T(8,128)(2,1)S(1)}, u32[]{:S(2)}, u32[]{:S(2)}) async-start(bf16[16,24,4096]{2,1,0:T(8,128)(2,1)} %bitcast.82), calls=%async_computation.1 | async-start | bytes 6291456 | tf_op jit(solution)/shard_map/all_to_all | solution.py:89
  220.2 5.3 %fusion.5 = f32[384,4096]{1,0:T(8,128)S(1)} fusion(bf16[384,768]{1,0:T(8,128)(2,1)} %get-tuple-element.21, bf16[1,4096,768]{2,1,0:T(8,128)(2,1)} %param.12), kind=kOutput, calls=%fused_computation.14 | convolution fusion | flops 2415919104 | bytes 13172736 | tf_op jit(solution)/shard_map/dot_general | solution.py:8
  225.5 8.4 %add_convert_fusion = bf16[384,4096]{1,0:T(8,128)(2,1)} fusion(f32[384,4096]{1,0:T(8,128)S(1)} %fusion.5, bf16[384,768]{1,0:T(8,128)(2,1)S(1)} %copy-done.6, bf16[1,4096,768]{2,1,0:T(8,128)(2,1)} %param.11), kind=kOutput, calls=%fused_computation.22 | convolution fusion | flops 2419064832 | bytes 16318464 | tf_op jit(solution)/shard_map/dot_general | solution.py:8
  233.9 45.7 %all-to-all-done.1 = bf16[16,24,4096]{2,1,0:T(8,128)(2,1)S(1)} async-done(((bf16[16,24,4096]{2,1,0:T(8,128)(2,1)}), bf16[16,24,4096]{2,1,0:T(8,128)(2,1)S(1)}, u32[]{:S(2)}, u32[]{:S(2)}) %all-to-all-start.1) | async-done | bytes 3145760 | tf_op jit(solution)/shard_map/all_to_all | solution.py:89
  279.6 15.5 %all-to-all-start.3 = ((bf16[16,24,4096]{2,1,0:T(8,128)(2,1)}), bf16[16,24,4096]{2,1,0:T(8,128)(2,1)}, u32[]{:S(2)}, u32[]{:S(2)}) async-start(bf16[16,24,4096]{2,1,0:T(8,128)(2,1)} %bitcast.81), calls=%async_computation.3 | async-start | bytes 6291456 | tf_op jit(solution)/shard_map/all_to_all | solution.py:96
  295.1 3.2 gather_fusion.1
  298.3 3.0 fusion.18
  302.0 52.5 %all-to-all-done.3 = bf16[16,24,4096]{2,1,0:T(8,128)(2,1)} async-done(((bf16[16,24,4096]{2,1,0:T(8,128)(2,1)}), bf16[16,24,4096]{2,1,0:T(8,128)(2,1)}, u32[]{:S(2)}, u32[]{:S(2)}) %all-to-all-start.3) | async-done | bytes 3145760 | tf_op jit(solution)/shard_map/all_to_all | solution.py:96
  354.5 6.2 %gather_fusion.4 = bf16[256,4096]{1,0:T(8,128)(2,1)S(1)} fusion(bf16[384,4096]{1,0:T(8,128)(2,1)} %bitcast.14, s32[1024]{0:T(1024)S(1)} %pad_clamp_fusion.1), kind=kCustom, calls=%fused_computation.4 | custom fusion | bytes 4195328 | tf_op jit(solution)/shard_map/gather | solution.py:124
  365.1 4.7 %copy.21 = bf16[1,768,2048]{2,1,0:T(8,128)(2,1)} copy(bf16[1,768,2048]{1,2,0:T(8,128)(2,1)} %bitcast.78) | data formatting | bytes 6291456
  369.8 49.1 %reduce-scatter.3.cloned.1.call-done = bf16[2048,1536]{1,0:T(8,128)(2,1)} async-done(((bf16[4096,1536]{1,0:T(8,128)(2,1)}), bf16[2048,1536]{1,0:T(8,128)(2,1)}) %reduce-scatter.3.cloned.1.call-update) | async-done | bytes 6291472 | tf_op jit(solution)/shard_map/reduce_scatter | solution.py:106
  419.0 5.9 %slice_bitcast_fusion = (bf16[1,2048,768]{2,1,0:T(8,128)(2,1)}, bf16[1,2048,768]{2,1,0:T(8,128)(2,1)}) fusion(bf16[2048,1536]{1,0:T(8,128)(2,1)} %reduce-scatter.3.cloned.1.call-done), kind=kLoop, calls=%fused_computation.25 | loop fusion | bytes 12582912 | tf_op jit(solution)/shard_map/broadcast_in_dim | solution.py:131
  (50 shorter events, 21.0 us)
Async XLA Ops:
  22.1 66.8 %all-to-all-start.2 = ((bf16[16,24,4096]{2,1,0:T(8,128)(2,1)}), bf16[16,24,4096]{2,1,0:T(8,128)(2,1)S(1)}, u32[]{:S(2)}, u32[]{:S(2)}) async-start(bf16[16,24,4096]{2,1,0:T(8,128)(2,1)} %fusion), calls=%async_computation.2 | async-start | bytes 6291456 | tf_op jit(solution)/shard_map/all_to_all | solution.py:75
  88.8 74.9 %all-to-all-start = ((bf16[16,24,4096]{2,1,0:T(8,128)(2,1)}), bf16[16,24,4096]{2,1,0:T(8,128)(2,1)}, u32[]{:S(2)}, u32[]{:S(2)}) async-start(bf16[16,24,4096]{2,1,0:T(8,128)(2,1)} %bitcast.3), calls=%async_computation | async-start | bytes 6291456 | tf_op jit(solution)/shard_map/all_to_all | solution.py:68
  104.3 260.8 %reduce-scatter.5.cloned.1.call-start = ((), (), s32[]{:S(2)}) async-start(), calls=%async_computation.7 | async-start | bytes 9437184 | tf_op jit(solution)/shard_map/reduce_scatter | solution.py:114
  163.7 6.4 %copy-start.7 = (f32[384,768]{1,0:T(8,128)S(1)}, f32[384,768]{1,0:T(8,128)}, u32[]{:S(2)}) copy-start(f32[384,768]{1,0:T(8,128)} %fusion.1) | copy-start | bytes 3538948
  177.9 0.8 copy-start.3
  184.1 1.1 copy-start.2
  184.1 1.2 copy-start.5
  184.1 234.9 %reduce-scatter.3.cloned.1.call-start = ((), (), s32[]{:S(2)}) async-start(), calls=%async_computation.6 | async-start | bytes 18874368 | tf_op jit(solution)/shard_map/reduce_scatter | solution.py:106
  197.0 1.1 copy-start.4
  204.8 74.8 %all-to-all-start.1 = ((bf16[16,24,4096]{2,1,0:T(8,128)(2,1)}), bf16[16,24,4096]{2,1,0:T(8,128)(2,1)S(1)}, u32[]{:S(2)}, u32[]{:S(2)}) async-start(bf16[16,24,4096]{2,1,0:T(8,128)(2,1)} %bitcast.82), calls=%async_computation.1 | async-start | bytes 6291456 | tf_op jit(solution)/shard_map/all_to_all | solution.py:89
  220.2 5.3 %copy-start.6 = (bf16[384,768]{1,0:T(8,128)(2,1)S(1)}, bf16[384,768]{1,0:T(8,128)(2,1)}, u32[]{:S(2)}) copy-start(bf16[384,768]{1,0:T(8,128)(2,1)} %get-tuple-element.20) | copy-start | bytes 1769476
  279.6 74.9 %all-to-all-start.3 = ((bf16[16,24,4096]{2,1,0:T(8,128)(2,1)}), bf16[16,24,4096]{2,1,0:T(8,128)(2,1)}, u32[]{:S(2)}, u32[]{:S(2)}) async-start(bf16[16,24,4096]{2,1,0:T(8,128)(2,1)} %bitcast.81), calls=%async_computation.3 | async-start | bytes 6291456 | tf_op jit(solution)/shard_map/all_to_all | solution.py:96
  295.1 3.2 copy-start.1
  360.7 2.1 copy-start
Sparse Core Ops, SparseCore 0:
  184.2 87.7 reduce-scatter.4
  274.5 144.4 reduce-scatter.2
where the time goes:
time: 433 us; the launch traced here: 432 us
  waiting for transfers between devices  254 us (59%)
  matrix products  61 us (14%)
  starting transfers between devices  54.3 us (13%)
  local copies, waits for them, and re-layouts  39.2 us (9%)
  between operations  14.2 us (3%)
  other arithmetic  8.58 us (2%)
    all_to_all x1, waiting for transfers between devices, local(): lax.all_to_all(send_grads.reshape(flat_shape), ('outer', 'inner'), split_...  54.4 us
    all_to_all x1, waiting for transfers between devices, local(): lax.all_to_all(send_rows.reshape(flat_shape), ('outer', 'inner'), split_a...  52.8 us
    all_to_all x1, waiting for transfers between devices, local(): lax.all_to_all(pair_grad.reshape(flat_shape), ('outer', 'inner'), split_a...  52.5 us
    reduce_scatter x1, waiting for transfers between devices, local(): lax.psum_scatter(contract_first(columns, joined_grads).astype(jnp.bfloat1...  49.1 us
    all_to_all x1, waiting for transfers between devices, local(): lax.all_to_all(expert_out.reshape(flat_shape), ('outer', 'inner'), split_...  45.7 us
    dot_general x3, matrix products, contract_last(): lax.dot_general(left, right, (((1,), (1,)), ((), ())), preferred_element_...  20.1 us
    dot_general x2, matrix products, contract_first(): lax.dot_general(left, right, (((0,), (0,)), ((), ())), preferred_element_...  17 us
    all_to_all x1, starting transfers between devices, local(): lax.all_to_all(pair_grad.reshape(flat_shape), ('outer', 'inner'), split_a...  15.5 us
  transfers between devices with their start and end apart: 6, of which 5 were waited for; matrix products, arithmetic and copies ran while one was open for 15% of the time, Pallas kernels for 0%

commit v1 on v0

v1 whole, which is shorter than its diff:
```python
import jax
import jax.numpy as jnp
from jax import lax
from jax.sharding import PartitionSpec as P

PLANE = ("outer", "inner")


def dot(left, right, left_dim, right_dim):
    return lax.dot_general(
        left,
        right,
        (((left_dim,), (right_dim,)), ((), ())),
        preferred_element_type=jnp.float32,
    )


def exchange(block_for, count):
    me = lax.axis_index("dp")
    got = []
    for shift in range(1, count):
        pairs = [(q, (q + shift) % count) for q in range(count)]
        got.append(lax.ppermute(block_for((me + shift) % count), "dp", pairs))
    return got


def local(tokens, expert_ids, gate_values, upstream, w_gate, w_up, w_down):
    local_tokens, width = tokens.shape
    groups = lax.axis_size("dp")
    inner_count = lax.axis_size("inner")
    expert_count = lax.axis_size("outer") * inner_count
    me = lax.axis_index("dp")
    expert = lax.axis_index("outer") * inner_count + lax.axis_index("inner")
    share = width // groups
    gate_mat, up_mat, down_mat = w_gate[0], w_up[0], w_down[0]

    def plane_gather(value):
        return lax.all_gather(value, PLANE, axis=0, tiled=True)

    chosen = expert_ids[:, :, None] == jnp.arange(expert_count, dtype=jnp.int32)[None, None, :]
    gate_grid = jnp.sum(jnp.where(chosen, gate_values[:, :, None], 0.0), axis=1)

    all_tokens = plane_gather(tokens)
    all_gates = plane_gather(gate_grid)
    all_upstream = plane_gather(upstream)
    both = jnp.stack([tokens, upstream], axis=1)
    far = exchange(lambda j: lax.dynamic_slice_in_dim(both, j * share, share, 2), groups)
    far = [plane_gather(block) for block in far]

    is_mine = jnp.arange(expert_count, dtype=jnp.int32) == expert
    gate = jnp.sum(jnp.where(is_mine[None, :], all_gates, 0.0), axis=1, keepdims=True)

    gate_pre = dot(all_tokens, gate_mat, 1, 0)
    up_pre = dot(all_tokens, up_mat, 1, 0)
    grad_hidden = dot(all_upstream, down_mat, 1, 1)
    sigma = jax.nn.sigmoid(gate_pre)
    silu_value = gate_pre * sigma
    hidden = silu_value * up_pre
    slope = sigma * (1.0 + gate_pre * (1.0 - sigma))
    gate_dot = jnp.sum(hidden * grad_hidden, axis=1)
    scaled = gate * grad_hidden
    gated_hidden = (gate * hidden).astype(jnp.bfloat16)
    grad_gate_pre = (scaled * up_pre * slope).astype(jnp.bfloat16)
    grad_up_pre = (scaled * silu_value).astype(jnp.bfloat16)

    packed = jnp.concatenate([grad_gate_pre, grad_up_pre, gated_hidden], axis=1)
    far_packed = exchange(lambda j: packed, groups)

    part_out = dot(gated_hidden, down_mat, 1, 0).astype(jnp.bfloat16)
    output = lax.psum_scatter(part_out, PLANE, scatter_dimension=0, tiled=True)
    part_grad = (dot(grad_gate_pre, gate_mat, 1, 1) + dot(grad_up_pre, up_mat, 1, 1)).astype(
        jnp.bfloat16
    )
    grad_tokens = lax.psum_scatter(part_grad, PLANE, scatter_dimension=0, tiled=True)

    gate_dots = lax.all_gather(gate_dot, PLANE, axis=0, tiled=False)
    gate_dots = lax.dynamic_slice_in_dim(gate_dots, expert * local_tokens, local_tokens, 1)
    grad_gates = jnp.sum(jnp.where(chosen, gate_dots.T[:, None, :], 0.0), axis=2)

    ff = gate_mat.shape[1]
    rows = jnp.concatenate(
        [lax.dynamic_slice_in_dim(all_tokens, me * share, share, 1)]
        + [block[:, 0] for block in far],
        axis=0,
    )
    ups = jnp.concatenate(
        [lax.dynamic_slice_in_dim(all_upstream, me * share, share, 1)]
        + [block[:, 1] for block in far],
        axis=0,
    )
    every = jnp.concatenate([packed] + far_packed, axis=0)
    grad_w_gate = dot(rows, every[:, :ff], 0, 0).astype(jnp.bfloat16)[None]
    grad_w_up = dot(rows, every[:, ff : 2 * ff], 0, 0).astype(jnp.bfloat16)[None]
    grad_w_down = dot(every[:, 2 * ff :], ups, 0, 0).astype(jnp.bfloat16)[None]
    return (output, grad_tokens, grad_gates, grad_w_gate, grad_w_up, grad_w_down)


def solution(mesh):
    rows = P(("dp", "outer", "inner"), None)
    expert = P(("outer", "inner"), None, None)
    return jax.shard_map(
        local,
        mesh=mesh,
        in_specs=(rows, rows, rows, rows, expert, expert, expert),
        out_specs=(
            rows,
            rows,
            rows,
            P(("outer", "inner"), "dp", None),
            P(("outer", "inner"), "dp", None),
            P(("outer", "inner"), None, "dp"),
        ),
        check_vma=False,
    )
```

time: 433 us -> 328 us (0.76)
  waiting for transfers between devices: 254 us -> 184 us
  starting transfers between devices: 54.3 us -> 4.77 us
  blocking collectives: 0 us -> 37.5 us
  local copies, waits for them, and re-layouts: 39.2 us -> 8.34 us
  other arithmetic: 8.58 us -> 20.1 us
    all_to_all x4 -> x0, waiting for transfers between devices: 205 us -> none  [the longest x1 54.4 us: local(): lax.all_to_all(send_grads.reshape(flat_shape), ('outer', 'inner'), split_...]
    all_gather x0 -> x3, waiting for transfers between devices: none -> 81.5 us  [plane_gather(): return lax.all_gather(value, PLANE, axis=0, tiled=True)]
    all_to_all x4 -> x0, starting transfers between devices: 53.8 us -> none  [the longest x1 15.5 us: local(): lax.all_to_all(pair_grad.reshape(flat_shape), ('outer', 'inner'), split_a...]
    ppermute x0 -> x2, waiting for transfers between devices: none -> 51.3 us  [exchange(): got.append(lax.ppermute(block_for((me + shift) % count), 'dp', pairs))]
    all_gather x0 -> x2, blocking collectives: none -> 37.5 us  [the longest x1 19 us: local(): gate_dots = lax.all_gather(gate_dot, PLANE, axis=0, tiled=False)]
    gather x5 -> x0, local copies, waits for them, and re-layouts: 19.5 us -> none  [the longest x1 6.18 us: local(): back_grad.reshape(-1, width)[pair_slot]]
    concatenate x1 -> x2, other arithmetic: 0.01 us -> 14.9 us  [the longest x1 13.4 us: local(): every = jnp.concatenate([packed] + far_packed, axis=0)]
    unnamed x19, local copies, waits for them, and re-layouts: 9.03 us -> 0.84 us
  transfers between devices with their start and end apart: 6 -> 7, of which waited for: 5 -> 5; matrix products, arithmetic and copies ran while one was open for 15% -> 26% of each run, Pallas kernels for 0% -> 0%
where the time goes in v1:
time: 328 us; the launch traced here: 327 us
  waiting for transfers between devices  184 us (56%)
  matrix products  58.6 us (18%)
  blocking collectives  37.5 us (11%)
  other arithmetic  20.1 us (6%)
  between operations  13.9 us (4%)
  local copies, waits for them, and re-layouts  8.34 us (3%)
  starting transfers between devices  4.77 us (1%)
    all_gather x3, waiting for transfers between devices, plane_gather(): return lax.all_gather(value, PLANE, axis=0, tiled=True)  81.5 us
    dot_general x9, matrix products, dot(): lax.dot_general(left, right, (((left_dim,), (right_dim,)), ((), ())), pre...  58.6 us
    ppermute x2, waiting for transfers between devices, exchange(): got.append(lax.ppermute(block_for((me + shift) % count), 'dp', pairs))  51.3 us
    reduce_scatter x1, waiting for transfers between devices, local(): lax.psum_scatter(part_grad, PLANE, scatter_dimension=0, tiled=True)  50 us
    all_gather x1, blocking collectives, local(): gate_dots = lax.all_gather(gate_dot, PLANE, axis=0, tiled=False)  19 us
    all_gather x1, blocking collectives, plane_gather(): return lax.all_gather(value, PLANE, axis=0, tiled=True)  18.4 us
    concatenate x1, other arithmetic, local(): every = jnp.concatenate([packed] + far_packed, axis=0)  13.4 us
  transfers between devices with their start and end apart: 7, of which 5 were waited for; matrix products, arithmetic and copies ran while one was open for 26% of the time, Pallas kernels for 0%

profile of v1, /device:TPU:0, one launch (start us, length us, event | category | flops | bytes accessed | tf_op | source)
XLA Modules:
  0.0 327.3 jit_solution(5599391850743331920)
XLA Ops:
  9.7 3.0 collective-permute-start
  12.7 6.3 %collective-permute-done = bf16[32,2,2048]{2,0,1:T(8,128)(2,1)S(1)} collective-permute-done((bf16[32,2,2048]{2,0,1:T(8,128)(2,1)S(1)}, bf16[32,2,2048]{2,0,1:T(8,128)(2,1)S(1)}, u32[]{:S(2)}, u32[]{:S(2)}) %collective-permute-start) | collective-permute-done | bytes 262176 | tf_op jit(solution)/shard_map/ppermute | solution.py:23
  19.8 43.7 %all-gather.7.cloned.1.call-done = bf16[512,4096]{1,0:T(8,128)(2,1)} async-done(((bf16[32,4096]{1,0:T(8,128)(2,1)}), bf16[512,4096]{1,0:T(8,128)(2,1)}) %all-gather.7.cloned.1.call-update) | async-done | bytes 4194320 | tf_op jit(solution)/shard_map/all_gather | solution.py:38
  63.5 7.2 %fusion.6 = f32[512,768]{1,0:T(8,128)S(1)} fusion(bf16[512,4096]{1,0:T(8,128)(2,1)} %all-gather.7.cloned.1.call-done, bf16[1,4096,768]{2,1,0:T(8,128)(2,1)} %param.12), kind=kOutput, calls=%fused_computation.7 | convolution fusion | flops 3221225472 | bytes 12058624 | tf_op jit(solution)/shard_map/dot_general | solution.py:10
  70.7 6.2 %fusion.10 = f32[512,768]{1,0:T(8,128)S(1)} fusion(bf16[512,4096]{1,0:T(8,128)(2,1)S(1)} %copy-done.4, bf16[1,4096,768]{2,1,0:T(8,128)(2,1)} %param.11), kind=kOutput, calls=%fused_computation.11 | convolution fusion | flops 3221225472 | bytes 12058624 | tf_op jit(solution)/shard_map/dot_general | solution.py:10
  76.9 37.8 %all-gather.9.cloned.1.call-done = bf16[512,4096]{1,0:T(8,128)(2,1)} async-done(((bf16[32,4096]{1,0:T(8,128)(2,1)}), bf16[512,4096]{1,0:T(8,128)(2,1)}) %all-gather.9.cloned.1.call-update) | async-done | bytes 4194320 | tf_op jit(solution)/shard_map/all_gather | solution.py:38
  114.7 8.8 %multiply_reduce_fusion = (f32[512]{0:T(512)S(1)}, f32[512,768]{1,0:T(8,128)}) fusion(f32[512,768]{1,0:T(8,128)S(1)} %fusion.6, f32[512,768]{1,0:T(8,128)S(1)} %fusion.10, bf16[512,4096]{1,0:T(8,128)(2,1)} %all-gather.9.cloned.1.call-done, bf16[1,768,4096]{2,1,0:T(8,128)(2,1)} %param.13), kind=kOutput, calls=%fused_computation.32 | convolution fusion | flops 3223977472 | bytes 15206400 | tf_op jit(solution)/shard_map/dot_general | solution.py:10
  123.5 19.0 %all-gather.2 = f32[16,1,512]{2,1,0:T(1,128)S(1)} all-gather(f32[1,1,512]{2,1,0:T(1,128)S(1)} %bitcast.52), channel_id=2, replica_groups=mesh['dp'=2,'outer'=8,'inner'=2] {'outer','inner'}, dimensions={0}, use_global_device_ids=true | all-gather | bytes 34816 | tf_op jit(solution)/shard_map/all_gather | solution.py:76
  143.2 18.4 %all-gather.1 = f32[16,32,16]{1,2,0:T(8,128)S(1)} all-gather(f32[1,32,16]{1,2,0:T(8,128)S(1)} %bitcast.50), channel_id=1, replica_groups=mesh['dp'=2,'outer'=8,'inner'=2] {'outer','inner'}, dimensions={0}, use_global_device_ids=true | all-gather | bytes 34816 | tf_op jit(solution)/shard_map/all_gather | solution.py:38
  161.9 3.4 %multiply_convert_fusion.1 = (bf16[512,768]{1,0:T(8,128)(2,1)S(1)}, bf16[512,768]{1,0:T(8,128)(2,1)S(1)}, bf16[512,768]{1,0:T(8,128)(2,1)S(1)}) fusion(f32[512,768]{1,0:T(8,128)} %copy-done.3, f32[512,768]{1,0:T(8,128)} %copy-done.2, f32[512,768]{1,0:T(8,128)} %get-tuple-element.14, f32[512]{0:T(512)S(1)} %select_reduce_fusion.2), kind=kLoop, calls=%fused_computation.34 | loop fusion | flops 6684672 | bytes 7079936 | tf_op jit(solution)/shard_map/convert_element_type | solution.py:63
  165.4 7.7 %fusion.12 = bf16[512,4096]{1,0:T(8,128)(2,1)} fusion(bf16[512,768]{1,0:T(8,128)(2,1)S(1)} %get-tuple-element.12, bf16[1,768,4096]{2,1,0:T(8,128)(2,1)} %param.13), kind=kOutput, calls=%fused_computation.13 | convolution fusion | flops 3223322624 | bytes 11272192 | tf_op jit(solution)/shard_map/dot_general | solution.py:10
  173.4 5.6 %fusion.4 = f32[512,4096]{1,0:T(8,128)S(1)} fusion(bf16[512,768]{1,0:T(8,128)(2,1)S(1)} %get-tuple-element.11, bf16[1,4096,768]{2,1,0:T(8,128)(2,1)} %param.12), kind=kOutput, calls=%fused_computation.5 | convolution fusion | flops 3221225472 | bytes 15466496 | tf_op jit(solution)/shard_map/dot_general | solution.py:10
  178.9 8.3 %add_convert_fusion = bf16[512,4096]{1,0:T(8,128)(2,1)} fusion(f32[512,4096]{1,0:T(8,128)S(1)} %fusion.4, bf16[512,768]{1,0:T(8,128)(2,1)S(1)} %get-tuple-element.10, bf16[1,4096,768]{2,1,0:T(8,128)(2,1)} %param.11), kind=kOutput, calls=%fused_computation | convolution fusion | flops 3225419776 | bytes 19660800 | tf_op jit(solution)/shard_map/dot_general | solution.py:10
  187.2 1.6 pad_maximum_fusion.4
  188.8 1.4 collective-permute-start.1
  190.2 3.4 %constant_dynamic-slice_fusion.1 = bf16[512,2048]{1,0:T(8,128)(2,1)} fusion(bf16[512,4096]{1,0:T(8,128)(2,1)} %all-gather.7.cloned.1.call-done, s32[]{:T(128)S(6)} %select_n.33), kind=kLoop, calls=%fused_computation.46 | loop fusion | bytes 4194308 | tf_op jit(solution)/shard_map/dynamic_slice | solution.py:82
  193.6 1.5 constant_dynamic-slice_fusion
  195.0 2.5 slice_bitcast_fusion
  197.6 45.0 %collective-permute-done.1 = bf16[512,2304]{1,0:T(8,128)(2,1)} collective-permute-done((bf16[512,2304]{1,0:T(8,128)(2,1)}, bf16[512,2304]{1,0:T(8,128)(2,1)}, u32[]{:S(2)}, u32[]{:S(2)}) %collective-permute-start.1) | collective-permute-done | bytes 2359328 | tf_op jit(solution)/shard_map/ppermute | solution.py:23
  242.6 13.4 %pad_maximum_fusion = bf16[1024,2304]{1,0:T(8,128)(2,1)S(1)} fusion(bf16[512,2304]{1,0:T(8,128)(2,1)} %collective-permute-done.1, bf16[512,768]{1,0:T(8,128)(2,1)S(1)} %get-tuple-element.12, bf16[512,768]{1,0:T(8,128)(2,1)S(1)} %get-tuple-element.11, bf16[512,768]{1,0:T(8,128)(2,1)S(1)} %get-tuple-element.10), kind=kLoop, calls=%fused_computation.14 | loop fusion | flops 18874368 | bytes 9437184 | tf_op jit(solution)/shard_map/concatenate | solution.py:91
  255.9 5.0 %fusion.25 = bf16[1,2048,768]{2,1,0:T(8,128)(2,1)} fusion(bf16[512,2048]{1,0:T(8,128)(2,1)S(1)} %get-tuple-element.9, bf16[512,2048]{1,0:T(8,128)(2,1)S(1)} %copy-done.1, bf16[1024,2304]{1,0:T(8,128)(2,1)S(1)} %pad_maximum_fusion), kind=kOutput, calls=%fused_computation.24 | convolution fusion | flops 3231186944 | bytes 8912896 | tf_op jit(solution)/shard_map/dot_general | solution.py:10
  261.0 5.0 %fusion.24 = bf16[1,2048,768]{2,1,0:T(8,128)(2,1)} fusion(bf16[512,2048]{1,0:T(8,128)(2,1)S(1)} %get-tuple-element.9, bf16[512,2048]{1,0:T(8,128)(2,1)S(1)} %copy-done.1, bf16[1024,2304]{1,0:T(8,128)(2,1)S(1)} %pad_maximum_fusion), kind=kOutput, calls=%fused_computation.23 | convolution fusion | flops 3231186944 | bytes 8912896 | tf_op jit(solution)/shard_map/dot_general | solution.py:10
  266.0 4.9 %fusion.26 = bf16[1,768,2048]{2,1,0:T(8,128)(2,1)} fusion(bf16[512,2048]{1,0:T(8,128)(2,1)S(1)} %get-tuple-element.8, bf16[512,2048]{1,0:T(8,128)(2,1)S(1)} %copy-done, bf16[1024,2304]{1,0:T(8,128)(2,1)S(1)} %pad_maximum_fusion), kind=kOutput, calls=%fused_computation.25 | convolution fusion | flops 3231186944 | bytes 8912896 | tf_op jit(solution)/shard_map/dot_general | solution.py:10
  270.8 50.0 %reduce-scatter.5.cloned.1.call-done = bf16[32,4096]{1,0:T(8,128)(2,1)} async-done(((bf16[512,4096]{1,0:T(8,128)(2,1)}), bf16[32,4096]{1,0:T(8,128)(2,1)}) %reduce-scatter.5.cloned.1.call-update) | async-done | bytes 262160 | tf_op jit(solution)/shard_map/reduce_scatter | solution.py:74
  (37 shorter events, 4.5 us)
Async XLA Ops:
  7.2 56.3 %all-gather.7.cloned.1.call-start = ((), (), s32[]{:S(2)}) async-start(), calls=%async_computation.2 | async-start | bytes 4456448 | tf_op jit(solution)/shard_map/all_gather | solution.py:38
  7.9 106.8 %all-gather.9.cloned.1.call-start = ((), (), s32[]{:S(2)}) async-start(), calls=%async_computation.4 | async-start | bytes 4456448 | tf_op jit(solution)/shard_map/all_gather | solution.py:38
  8.6 186.4 %all-gather.11.cloned.1.call-start = ((), (), s32[]{:S(2)}) async-start(), calls=%async_computation.6 | async-start | bytes 4456448 | tf_op jit(solution)/shard_map/all_gather | solution.py:38
  9.7 9.3 %collective-permute-start = (bf16[32,2,2048]{2,0,1:T(8,128)(2,1)S(1)}, bf16[32,2,2048]{2,0,1:T(8,128)(2,1)S(1)}, u32[]{:S(2)}, u32[]{:S(2)}) collective-permute-start(bf16[32,2,2048]{2,0,1:T(8,128)(2,1)S(1)} %fusion.33), channel_id=1, source_target_pairs={{0,16},{16,0},{1,17},{17,1},{2,18},{18,2},{3,19},{19,3},{4,20},{20... | collective-permute-start | bytes 786440 | tf_op jit(solution)/shard_map/ppermute | solution.py:23
  19.0 0.7 copy-start.6
  19.7 251.1 %reduce-scatter.3.cloned.1.call-start = ((), (), s32[]{:S(2)}) async-start(), calls=%async_computation.3 | async-start | bytes 4456448 | tf_op jit(solution)/shard_map/reduce_scatter | solution.py:70
  63.5 7.2 %copy-start.4 = (bf16[512,4096]{1,0:T(8,128)(2,1)S(1)}, bf16[512,4096]{1,0:T(8,128)(2,1)}, u32[]{:S(2)}) copy-start(bf16[512,4096]{1,0:T(8,128)(2,1)} %all-gather.7.cloned.1.call-done) | copy-start | bytes 12582916
  70.7 44.1 %copy-start.2 = (f32[512,768]{1,0:T(8,128)}, f32[512,768]{1,0:T(8,128)S(1)}, u32[]{:S(2)}) copy-start(f32[512,768]{1,0:T(8,128)S(1)} %fusion.6) | copy-start | bytes 4718596
  76.9 46.6 %copy-start.3 = (f32[512,768]{1,0:T(8,128)}, f32[512,768]{1,0:T(8,128)S(1)}, u32[]{:S(2)}) copy-start(f32[512,768]{1,0:T(8,128)S(1)} %fusion.10) | copy-start | bytes 4718596
  76.9 65.7 %copy-start.7 = (s32[32,8]{0,1:T(8,128)S(1)}, s32[32,8]{0,1:T(8,128)}, u32[]{:S(2)}) copy-start(s32[32,8]{0,1:T(8,128)} %param.8) | copy-start | bytes 3076
  76.9 65.7 %copy-start.8 = (f32[32,8]{0,1:T(8,128)S(1)}, f32[32,8]{0,1:T(8,128)}, u32[]{:S(2)}) copy-start(f32[32,8]{0,1:T(8,128)} %param.9) | copy-start | bytes 3076
  173.1 147.7 %reduce-scatter.5.cloned.1.call-start = ((), (), s32[]{:S(2)}) async-start(), calls=%async_computation.5 | async-start | bytes 4456448 | tf_op jit(solution)/shard_map/reduce_scatter | solution.py:74
  188.8 53.8 %collective-permute-start.1 = (bf16[512,2304]{1,0:T(8,128)(2,1)}, bf16[512,2304]{1,0:T(8,128)(2,1)}, u32[]{:S(2)}, u32[]{:S(2)}) collective-permute-start(bf16[512,2304]{1,0:T(8,128)(2,1)} %pad_maximum_fusion.4), channel_id=1, source_target_pairs={{0,16},{16,0},{1,17},{17,1},{2,18},{18,2},{3,19},{19,3},{4,20},{20... | collective-permute-start | bytes 7077896 | tf_op jit(solution)/shard_map/ppermute | solution.py:23
  190.2 3.4 %copy-start.5 = (bf16[512,4096]{1,0:T(8,128)(2,1)S(1)}, bf16[512,4096]{1,0:T(8,128)(2,1)}, u32[]{:S(2)}) copy-start(bf16[512,4096]{1,0:T(8,128)(2,1)} %all-gather.9.cloned.1.call-done) | copy-start | bytes 12582916
  197.6 58.4 %copy-start.1 = (bf16[512,2048]{1,0:T(8,128)(2,1)S(1)}, bf16[512,2048]{1,0:T(8,128)(2,1)}, u32[]{:S(2)}) copy-start(bf16[512,2048]{1,0:T(8,128)(2,1)} %constant_dynamic-slice_fusion.1) | copy-start | bytes 6291460
  261.0 5.0 %copy-start = (bf16[512,2048]{1,0:T(8,128)(2,1)S(1)}, bf16[512,2048]{1,0:T(8,128)(2,1)}, u32[]{:S(2)}) copy-start(bf16[512,2048]{1,0:T(8,128)(2,1)} %constant_dynamic-slice_fusion) | copy-start | bytes 6291460
Sparse Core Ops, SparseCore 0:
  10.2 53.2 all-gather.6
  65.6 49.0 all-gather.8
  116.9 49.6 all-gather.10
  173.2 70.9 reduce-scatter.2
  249.0 71.7 reduce-scatter.4

commit v2 on v1

--- a/solution.py
+++ b/solution.py
@@ -1,6 +1,10 @@
+import functools
+
 import jax
 import jax.numpy as jnp
 from jax import lax
+from jax.experimental import pallas as pl
+from jax.experimental.pallas import tpu as pltpu
 from jax.sharding import PartitionSpec as P
 
 PLANE = ("outer", "inner")
@@ -13,6 +17,318 @@
         (((left_dim,), (right_dim,)), ((), ())),
         preferred_element_type=jnp.float32,
     )
+
+
+MESH = pl.DeviceIdType.MESH
+VMEM_LIMIT = 48 * 1024 * 1024
+
+
+def place(sizes):
+    highs, lows, _ = sizes
+    outer = lax.axis_index("outer")
+    return lax.axis_index("dp"), outer // lows, outer % lows, lax.axis_index("inner")
+
+
+def greet(sizes):
+    highs, lows, cores = sizes
+    dp, hi, lo, core = place(sizes)
+    peers = [(dp, (hi + d) % highs * lows + lo, core) for d in range(1, highs)]
+    peers += [(dp, hi * lows + (lo + d) % lows, core) for d in range(1, lows)]
+    peers += [(dp, hi * lows + lo, (core + d) % cores) for d in range(1, cores)]
+    barrier = pltpu.get_barrier_semaphore()
+    for peer in peers:
+        pl.semaphore_signal(barrier, inc=1, device_id=peer, device_id_type=MESH)
+    pl.semaphore_wait(barrier, len(peers))
+
+
+def gather_kernel(sizes, chunks, *refs):
+    highs, lows, cores = sizes
+    count = len(refs) - 7
+    sources, results = refs[: count // 2], refs[count // 2 : count]
+    own_sem, hi_send, hi_recv, lo_send, lo_recv, core_send, core_recv = refs[count:]
+    dp, hi, lo, core = place(sizes)
+    mine = (hi * lows + lo) * cores + core
+    greet(sizes)
+
+    def block_of(high, low, at_core):
+        return (high * lows + low) * cores + at_core
+
+    def copy(src, dst, send, recv, outer, at_core):
+        return pltpu.make_async_remote_copy(
+            src_ref=src,
+            dst_ref=dst,
+            send_sem=send,
+            recv_sem=recv,
+            device_id=(dp, outer, at_core),
+            device_id_type=MESH,
+        )
+
+    def to_hi(c, d):
+        which, cols = chunks[c]
+        return copy(
+            sources[which].at[:, cols],
+            results[which].at[mine, :, cols],
+            hi_send.at[c, d],
+            hi_recv.at[c, d],
+            (hi + d) % highs * lows + lo,
+            core,
+        )
+
+    def to_lo(c, d, h):
+        which, cols = chunks[c]
+        at = block_of((hi + highs - h) % highs, lo, core)
+        src = sources[which].at[:, cols] if h == 0 else results[which].at[at, :, cols]
+        return copy(
+            src,
+            results[which].at[at, :, cols],
+            lo_send.at[c, d, h],
+            lo_recv.at[c, d, h],
+            hi * lows + (lo + d) % lows,
+            core,
+        )
+
+    def to_core(c, d, h, e):
+        which, cols = chunks[c]
+        at = block_of((hi + highs - h) % highs, (lo + lows - d) % lows, core)
+        src = sources[which].at[:, cols] if h == 0 and d == 0 else results[which].at[at, :, cols]
+        return copy(
+            src,
+            results[which].at[at, :, cols],
+            core_send.at[c, d, h, e],
+            core_recv.at[c, d, h, e],
+            hi * lows + lo,
+            (core + e) % cores,
+        )
+
+    sent = []
+
+    def start(what):
+        what.start()
+        sent.append(what)
+
+    for c in range(len(chunks)):
+        for d in range(1, lows):
+            start(to_lo(c, d, 0))
+        for d in range(1, highs):
+            start(to_hi(c, d))
+        for e in range(1, cores):
+            start(to_core(c, 0, 0, e))
+    kept = [
+        pltpu.make_async_copy(sources[w], results[w].at[mine], own_sem.at[w])
+        for w in range(count // 2)
+    ]
+    for one in kept:
+        one.start()
+    for c in range(len(chunks)):
+        for h in range(1, highs):
+            to_hi(c, h).wait_recv()
+            for d in range(1, lows):
+                start(to_lo(c, d, h))
+            for e in range(1, cores):
+                start(to_core(c, 0, h, e))
+        for h in range(highs):
+            for d in range(1, lows):
+                to_lo(c, d, h).wait_recv()
+                for e in range(1, cores):
+                    start(to_core(c, d, h, e))
+    for c in range(len(chunks)):
+        for h in range(highs):
+            for d in range(lows):
+                for e in range(1, cores):
+                    to_core(c, d, h, e).wait_recv()
+    for one in kept:
+        one.wait()
+    for one in sent:
+        one.wait_send()
+
+
+def plane_sizes():
+    outer = lax.axis_size("outer")
+    highs = 4 if outer % 4 == 0 else 1
+    return highs, outer // highs, lax.axis_size("inner")
+
+
+def cut(arrays, width):
+    chunks = []
+    for which, value in enumerate(arrays):
+        for first in range(0, value.shape[-1], width):
+            chunks.append((which, pl.ds(first, min(width, value.shape[-1] - first))))
+    return chunks
+
+
+def gather_plane(arrays, width):
+    sizes = highs, lows, cores = plane_sizes()
+    blocks = highs * lows * cores
+    chunks = cut(arrays, width)
+    n = len(chunks)
+    dma = pltpu.SemaphoreType.DMA
+    got = pl.pallas_call(
+        functools.partial(gather_kernel, sizes, chunks),
+        out_shape=[jax.ShapeDtypeStruct((blocks,) + a.shape, a.dtype) for a in arrays],
+        in_specs=[pl.BlockSpec(memory_space=pl.ANY)] * len(arrays),
+        out_specs=[pl.BlockSpec(memory_space=pl.ANY)] * len(arrays),
+        scratch_shapes=[
+            dma((len(arrays),)),
+            dma((n, highs)),
+            dma((n, highs)),
+            dma((n, lows, highs)),
+            dma((n, lows, highs)),
+            dma((n, lows, highs, cores)),
+            dma((n, lows, highs, cores)),
+        ],
+        compiler_params=pltpu.CompilerParams(collective_id=0, has_side_effects=True),
+        cost_estimate=pl.CostEstimate(flops=0, bytes_accessed=150_000_000, transcendentals=0),
+    )(*arrays)
+    return [g.reshape((-1,) + g.shape[2:]) for g in got]
+
+
+def scatter_kernel(sizes, chunks, count, *refs):
+    highs, lows, cores = sizes
+    n = len(chunks)
+    sources, results = refs[:count], refs[count : 2 * count]
+    held, from_core, from_lo, half, from_hi = (
+        refs[2 * count + n * k : 2 * count + n * (k + 1)] for k in range(5)
+    )
+    load_sem, core_send, core_recv, lo_send, lo_recv, hi_send, hi_recv = refs[2 * count + 5 * n :]
+    dp, hi, lo, core = place(sizes)
+    greet(sizes)
+
+    def copy(src, dst, send, recv, outer, at_core):
+        return pltpu.make_async_remote_copy(
+            src_ref=src,
+            dst_ref=dst,
+            send_sem=send,
+            recv_sem=recv,
+            device_id=(dp, outer, at_core),
+            device_id_type=MESH,
+        )
+
+    def load(c):
+        which, cols = chunks[c]
+        return pltpu.make_async_copy(
+            sources[which].at[:, :, core, :, cols], held[c], load_sem.at[c]
+        )
+
+    def to_core(c, e):
+        which, cols = chunks[c]
+        return copy(
+            sources[which].at[:, :, (core + e) % cores, :, cols],
+            from_core[c].at[e - 1],
+            core_send.at[c, e],
+            core_recv.at[c, e],
+            hi * lows + lo,
+            (core + e) % cores,
+        )
+
+    def to_lo(c, d):
+        return copy(
+            held[c].at[:, (lo + d) % lows],
+            from_lo[c].at[d - 1],
+            lo_send.at[c, d],
+            lo_recv.at[c, d],
+            hi * lows + (lo + d) % lows,
+            core,
+        )
+
+    def to_hi(c, d):
+        return copy(
+            half[c].at[(hi + d) % highs],
+            from_hi[c].at[d - 1],
+            hi_send.at[c, d],
+            hi_recv.at[c, d],
+            (hi + d) % highs * lows + lo,
+            core,
+        )
+
+    def over_cores(c):
+        load(c).wait()
+        for e in range(1, cores):
+            to_core(c, e).wait_recv()
+        for h in range(highs):
+            for l in range(lows):
+                total = held[c][h, l].astype(jnp.float32)
+                for e in range(1, cores):
+                    total += from_core[c][e - 1, h, l].astype(jnp.float32)
+                held[c][h, l] = total.astype(held[c].dtype)
+        for d in range(1, lows):
+            to_lo(c, d).start()
+
+    def over_lo(c):
+        for d in range(1, lows):
+            to_lo(c, d).wait_recv()
+        for h in range(highs):
+            total = held[c][h, lo].astype(jnp.float32)
+            for d in range(1, lows):
+                total += from_lo[c][d - 1, h].astype(jnp.float32)
+            half[c][h] = total.astype(half[c].dtype)
+        for d in range(1, highs):
+            to_hi(c, d).start()
+
+    def over_hi(c):
+        which, cols = chunks[c]
+        for d in range(1, highs):
+            to_hi(c, d).wait_recv()
+        total = half[c][hi].astype(jnp.float32)
+        for d in range(1, highs):
+            total += from_hi[c][d - 1].astype(jnp.float32)
+        results[which][:, cols] = total.astype(results[which].dtype)
+
+    for c in range(n):
+        for e in range(1, cores):
+            to_core(c, e).start()
+        load(c).start()
+    for step in range(n + 4):
+        if step < n:
+            over_cores(step)
+        if 0 <= step - 2 < n:
+            over_lo(step - 2)
+        if 0 <= step - 4:
+            over_hi(step - 4)
+    for c in range(n):
+        for e in range(1, cores):
+            to_core(c, e).wait_send()
+        for d in range(1, lows):
+            to_lo(c, d).wait_send()
+        for d in range(1, highs):
+            to_hi(c, d).wait_send()
+
+
+def scatter_plane(arrays, width):
+    sizes = highs, lows, cores = plane_sizes()
+    rows = arrays[0].shape[0] // (highs * lows * cores)
+    arrays = [a.reshape(highs, lows, cores, rows, a.shape[-1]) for a in arrays]
+    chunks = cut(arrays, width)
+    n = len(chunks)
+    dma = pltpu.SemaphoreType.DMA
+    kinds = [(arrays[which].dtype, cols.size) for which, cols in chunks]
+
+    def buffers(*lead):
+        return [pltpu.VMEM(lead + (rows, w), t) for t, w in kinds]
+
+    return pl.pallas_call(
+        functools.partial(scatter_kernel, sizes, chunks, len(arrays)),
+        out_shape=[jax.ShapeDtypeStruct((rows, a.shape[-1]), a.dtype) for a in arrays],
+        in_specs=[pl.BlockSpec(memory_space=pl.ANY)] * len(arrays),
+        out_specs=[pl.BlockSpec(memory_space=pltpu.VMEM)] * len(arrays),
+        scratch_shapes=[
+            *buffers(highs, lows),
+            *buffers(max(cores - 1, 1), highs, lows),
+            *buffers(max(lows - 1, 1), highs),
+            *buffers(highs),
+            *buffers(max(highs - 1, 1)),
+            dma((n,)),
+            dma((n, cores)),
+            dma((n, cores)),
+            dma((n, lows)),
+            dma((n, lows)),
+            dma((n, highs)),
+            dma((n, highs)),
+        ],
+        compiler_params=pltpu.CompilerParams(
+            collective_id=1, has_side_effects=True, vmem_limit_bytes=VMEM_LIMIT
+        ),
+        cost_estimate=pl.CostEstimate(flops=0, bytes_accessed=180_000_000, transcendentals=0),
+    )(*arrays)
 
 
 def exchange(block_for, count):
@@ -40,11 +356,12 @@
     chosen = expert_ids[:, :, None] == jnp.arange(expert_count, dtype=jnp.int32)[None, None, :]
     gate_grid = jnp.sum(jnp.where(chosen, gate_values[:, :, None], 0.0), axis=1)
 
-    all_tokens = plane_gather(tokens)
-    all_gates = plane_gather(gate_grid)
-    all_upstream = plane_gather(upstream)
+    lanes = jnp.pad(gate_grid, ((0, 0), (0, -expert_count % 128)))
+    all_gates, all_tokens, all_upstream = gather_plane([lanes, tokens, upstream], 2048)
+    all_gates = all_gates[:, :expert_count]
     both = jnp.stack([tokens, upstream], axis=1)
     far = exchange(lambda j: lax.dynamic_slice_in_dim(both, j * share, share, 2), groups)
+    *far, all_gates = lax.optimization_barrier((*far, all_gates))
     far = [plane_gather(block) for block in far]
 
     is_mine = jnp.arange(expert_count, dtype=jnp.int32) == expert
@@ -67,15 +384,13 @@
     far_packed = exchange(lambda j: packed, groups)
 
     part_out = dot(gated_hidden, down_mat, 1, 0).astype(jnp.bfloat16)
-    output = lax.psum_scatter(part_out, PLANE, scatter_dimension=0, tiled=True)
     part_grad = (dot(grad_gate_pre, gate_mat, 1, 1) + dot(grad_up_pre, up_mat, 1, 1)).astype(
         jnp.bfloat16
     )
-    grad_tokens = lax.psum_scatter(part_grad, PLANE, scatter_dimension=0, tiled=True)
-
-    gate_dots = lax.all_gather(gate_dot, PLANE, axis=0, tiled=False)
-    gate_dots = lax.dynamic_slice_in_dim(gate_dots, expert * local_tokens, local_tokens, 1)
-    grad_gates = jnp.sum(jnp.where(chosen, gate_dots.T[:, None, :], 0.0), axis=2)
+    lane = jnp.arange(lanes.shape[1], dtype=jnp.int32)
+    dots = jnp.where(lane[None, :] == expert, gate_dot[:, None], 0.0)
+    dots, output, grad_tokens = scatter_plane([dots, part_out, part_grad], 1024)
+    grad_gates = jnp.sum(jnp.where(chosen, dots[:, None, :expert_count], 0.0), axis=2)
 
     ff = gate_mat.shape[1]
     rows = jnp.concatenate(

time: 328 us -> 231 us (0.70)
  waiting for transfers between devices: 184 us -> 0.02 us
  Pallas kernels: 0 us -> 127 us
  blocking collectives: 37.5 us -> 0 us
  matrix products: 58.6 us -> 53.1 us
  local copies, waits for them, and re-layouts: 8.34 us -> 12.3 us
    pallas_call x0 -> x2, Pallas kernels: none -> 127 us  [the longest x1 63.9 us: gather_plane(): pl.pallas_call(functools.partial(gather_kernel, sizes, chunks), out_shape...]
    all_gather x3 -> x1, waiting for transfers between devices: 81.5 us -> 0.01 us  [plane_gather(): return lax.all_gather(value, PLANE, axis=0, tiled=True)]
    ppermute x2, waiting for transfers between devices: 51.3 us -> 0.01 us  [exchange(): got.append(lax.ppermute(block_for((me + shift) % count), 'dp', pairs))]
    reduce_scatter x2 -> x0, waiting for transfers between devices: 50 us -> none  [the longest x1 50 us: local(): lax.psum_scatter(part_grad, PLANE, scatter_dimension=0, tiled=True)]
    all_gather x2 -> x0, blocking collectives: 37.5 us -> none  [the longest x1 19 us: local(): gate_dots = lax.all_gather(gate_dot, PLANE, axis=0, tiled=False)]
    dot_general x9, matrix products: 58.6 us -> 53.1 us  [dot(): lax.dot_general(left, right, (((left_dim,), (right_dim,)), ((), ())), pre...]
    dynamic_slice x1, local copies, waits for them, and re-layouts: 1.45 us -> 5.1 us  [local(): lax.dynamic_slice_in_dim(all_upstream, me * share, share, 1)]
    dynamic_slice x2 -> x0, local copies, waits for them, and re-layouts: 3.47 us -> none  [the longest x1 3.39 us: local(): lax.dynamic_slice_in_dim(all_tokens, me * share, share, 1)]
  transfers between devices with their start and end apart: 7 -> 3, of which waited for: 5 -> 0; matrix products, arithmetic and copies ran while one was open for 26% -> 27% of each run, Pallas kernels for 0% -> 55%
where the time goes in v2:
time: 231 us
  Pallas kernels  127 us (55%)
  matrix products  53.1 us (23%)
  other arithmetic  20 us (9%)
  between operations  14.3 us (6%)
  local copies, waits for them, and re-layouts  12.3 us (5%)
  starting transfers between devices  3.58 us (2%)
    pallas_call x1, Pallas kernels, gather_plane(): pl.pallas_call(functools.partial(gather_kernel, sizes, chunks), out_shape...  63.9 us
    pallas_call x1, Pallas kernels, scatter_plane(): pl.pallas_call(functools.partial(scatter_kernel, sizes, chunks, len(array...  63.5 us
    dot_general x9, matrix products, dot(): lax.dot_general(left, right, (((left_dim,), (right_dim,)), ((), ())), pre...  53.1 us
    concatenate x1, other arithmetic, local(): every = jnp.concatenate([packed] + far_packed, axis=0)  15.8 us
    dynamic_slice x1, local copies, waits for them, and re-layouts, local(): lax.dynamic_slice_in_dim(all_upstream, me * share, share, 1)  5.1 us
  transfers between devices with their start and end apart: 3, of which 0 were waited for; matrix products, arithmetic and copies ran while one was open for 27% of the time, Pallas kernels for 55%

profile of v2, /device:TPU:0, one launch (start us, length us, event | category | flops | bytes accessed | tf_op | source)
XLA Modules:
  0.0 230.6 jit_solution(17967374347127668177)
XLA Ops:
  7.2 1.0 fusion.33
  8.2 3.0 %collective-permute-start = (bf16[32,2,2048]{2,0,1:T(8,128)(2,1)S(1)}, bf16[32,2,2048]{2,0,1:T(8,128)(2,1)S(1)}, u32[]{:S(2)}, u32[]{:S(2)}) collective-permute-start(bf16[32,2,2048]{2,0,1:T(8,128)(2,1)S(1)} %fusion.33), channel_id=1, source_target_pairs={{0,16},{16,0},{1,17},{17,1},{2,18},{18,2},{3,19},{19,3},{4,20},{20... | collective-permute-start | bytes 786440 | tf_op jit(solution)/shard_map/ppermute | solution.py:339
  11.2 0.7 select_reduce_fusion.2
  12.0 0.6 pad.4.refs_0_
  12.6 63.9 %shard_map.118 = (f32[16,32,128]{2,1,0:T(8,128)}, bf16[16,32,4096]{2,1,0:T(8,128)(2,1)}, bf16[16,32,4096]{2,1,0:T(8,128)(2,1)}) custom-call(f32[32,128]{1,0:T(8,128)} %pad.4.refs_0_, bf16[32,4096]{1,0:T(8,128)(2,1)} %refs_1_.1, bf16[32,4096]{1,0:T(8,128)(2,1)} %refs_2_.1), custom_call_target="tpu_custom_call" | custom-call | bytes 150000000 | tf_op jit(solution)/shard_map/pallas_call | solution.py:165
  76.5 0.7 copy-done.5
  77.3 5.1 %constant_dynamic-slice_fusion = (bf16[512,2048]{1,0:T(8,128)(2,1)}, bf16[512,2048]{1,0:T(8,128)(2,1)}) fusion(bf16[512,4096]{1,0:T(8,128)(2,1)} %bitcast.54, s32[]{:T(128)S(6)} %select_n.37, bf16[512,4096]{1,0:T(8,128)(2,1)} %bitcast.51), kind=kLoop, calls=%fused_computation.46 | loop fusion | bytes 8388612 | tf_op jit(solution)/shard_map/dynamic_slice | solution.py:402
  82.5 7.5 %fusion.6 = f32[512,768]{1,0:T(8,128)} fusion(bf16[512,4096]{1,0:T(8,128)(2,1)S(1)} %bitcast.52, bf16[1,4096,768]{2,1,0:T(8,128)(2,1)} %param.12), kind=kOutput, calls=%fused_computation.7 | convolution fusion | flops 3221225472 | bytes 12058624 | tf_op jit(solution)/shard_map/dot_general | solution.py:14
  90.0 3.7 %fusion.2 = f32[512,768]{1,0:T(8,128)S(1)} fusion(bf16[512,4096]{1,0:T(8,128)(2,1)S(1)} %bitcast.55, bf16[1,768,4096]{2,1,0:T(8,128)(2,1)S(1)} %bitcast.60), kind=kOutput, calls=%fused_computation.3 | convolution fusion | flops 3221225472 | bytes 12058624 | tf_op jit(solution)/shard_map/dot_general | solution.py:14
  93.8 5.8 %multiply_convert_fusion.1 = (bf16[512,768]{1,0:T(8,128)(2,1)S(1)}, f32[512]{0:T(512)S(1)}, bf16[512,768]{1,0:T(8,128)(2,1)S(1)}, bf16[512,768]{1,0:T(8,128)(2,1)S(1)}) fusion(f32[512,768]{1,0:T(8,128)} %fusion.6, f32[512,768]{1,0:T(8,128)S(1)} %fusion.2, f32[512]{0:T(512)S(1)} %select_reduce_fusion, bf16[512,4096]{1,0:T(8,128)(2,1)S(1)} %bitcast.53, ...), kind=kOutput, calls=%fused_computation.33 | convolution fusion | flops 3228696064 | bytes 15994880 | tf_op jit(solution)/shard_map/dot_general | solution.py:14
  99.6 1.6 pad_maximum_fusion.4
  101.7 5.7 %fusion.4 = f32[512,4096]{1,0:T(8,128)} fusion(bf16[512,768]{1,0:T(8,128)(2,1)S(1)} %get-tuple-element.26, bf16[1,4096,768]{2,1,0:T(8,128)(2,1)S(1)} %bitcast.58), kind=kOutput, calls=%fused_computation.5 | convolution fusion | flops 3221225472 | bytes 15466496 | tf_op jit(solution)/shard_map/dot_general | solution.py:14
  107.7 6.4 %fusion.12 = bf16[512,4096]{1,0:T(8,128)(2,1)S(1)} fusion(bf16[512,768]{1,0:T(8,128)(2,1)S(1)} %get-tuple-element.27, bf16[1,768,4096]{2,1,0:T(8,128)(2,1)} %param.13), kind=kOutput, calls=%fused_computation.13 | convolution fusion | flops 3223322624 | bytes 11272192 | tf_op jit(solution)/shard_map/dot_general | solution.py:14
  114.1 9.1 %add_convert_fusion = bf16[512,4096]{1,0:T(8,128)(2,1)} fusion(f32[512,4096]{1,0:T(8,128)} %fusion.4, bf16[512,768]{1,0:T(8,128)(2,1)S(1)} %get-tuple-element.22, bf16[1,4096,768]{2,1,0:T(8,128)(2,1)} %param.11), kind=kOutput, calls=%fused_computation | convolution fusion | flops 3225419776 | bytes 19660800 | tf_op jit(solution)/shard_map/dot_general | solution.py:14
  123.2 63.5 %shard_map.119 = (f32[32,128]{1,0:T(8,128)S(1)}, bf16[32,4096]{1,0:T(8,128)(2,1)S(1)}, bf16[32,4096]{1,0:T(8,128)(2,1)S(1)}) custom-call(f32[4,2,2,32,128]{4,3,2,1,0:T(8,128)S(1)} %broadcast_select_fusion.refs_0_, bf16[4,2,2,32,4096]{4,3,2,1,0:T(8,128)(2,1)S(1)} %bitcast.46, bf16[4,2,2,32,4096]{4,3,2,1,0:T(8,128)(2,1)} %bitcast.48), custom_call_target="tpu_custom_call" | custom-call | bytes 180000000 | tf_op jit(solution)/shard_map/pallas_call | solution.py:308
  186.8 0.6 select_reduce_fusion.1
  187.4 15.8 %pad_maximum_fusion = bf16[1024,2304]{1,0:T(8,128)(2,1)} fusion(bf16[512,2304]{1,0:T(8,128)(2,1)} %collective-permute-done.1, bf16[512,768]{1,0:T(8,128)(2,1)S(1)} %get-tuple-element.27, bf16[512,768]{1,0:T(8,128)(2,1)S(1)} %get-tuple-element.26, bf16[512,768]{1,0:T(8,128)(2,1)S(1)} %get-tuple-element.22), kind=kLoop, calls=%fused_computation.14 | loop fusion | flops 18874368 | bytes 9437184 | tf_op jit(solution)/shard_map/concatenate | solution.py:406
  203.2 2.7 %slice_bitcast_fusion = (bf16[512,2048]{1,0:T(8,128)(2,1)S(1)}, bf16[512,2048]{1,0:T(8,128)(2,1)S(1)}) fusion(bf16[512,2,2048]{2,0,1:T(8,128)(2,1)} %all-gather.2.cloned.1.call-done), kind=kLoop, calls=%fused_computation.27 | loop fusion | bytes 8388608 | tf_op jit(solution)/shard_map/squeeze | solution.py:403
  206.1 1.4 copy-done
  207.5 5.0 %fusion.25 = bf16[1,2048,768]{2,1,0:T(8,128)(2,1)} fusion(bf16[512,2048]{1,0:T(8,128)(2,1)S(1)} %get-tuple-element.25, bf16[512,2048]{1,0:T(8,128)(2,1)S(1)} %copy-done.2, bf16[1024,2304]{1,0:T(8,128)(2,1)S(1)} %copy-done), kind=kOutput, calls=%fused_computation.24 | convolution fusion | flops 3231186944 | bytes 8912896 | tf_op jit(solution)/shard_map/dot_general | solution.py:14
  212.5 5.0 %fusion.24 = bf16[1,2048,768]{2,1,0:T(8,128)(2,1)} fusion(bf16[512,2048]{1,0:T(8,128)(2,1)S(1)} %get-tuple-element.25, bf16[512,2048]{1,0:T(8,128)(2,1)S(1)} %copy-done.2, bf16[1024,2304]{1,0:T(8,128)(2,1)S(1)} %copy-done), kind=kOutput, calls=%fused_computation.23 | convolution fusion | flops 3231186944 | bytes 8912896 | tf_op jit(solution)/shard_map/dot_general | solution.py:14
  217.5 4.9 %fusion.26 = bf16[1,768,2048]{2,1,0:T(8,128)(2,1)} fusion(bf16[512,2048]{1,0:T(8,128)(2,1)S(1)} %get-tuple-element.24, bf16[512,2048]{1,0:T(8,128)(2,1)S(1)} %copy-done.1, bf16[1024,2304]{1,0:T(8,128)(2,1)S(1)} %copy-done), kind=kOutput, calls=%fused_computation.25 | convolution fusion | flops 3231186944 | bytes 8912896 | tf_op jit(solution)/shard_map/dot_general | solution.py:14
  222.4 0.7 copy.19
  223.1 0.7 copy.20
  (42 shorter events, 1.3 us)
Async XLA Ops:
  7.2 196.1 %all-gather.2.cloned.1.call-start = ((), (), s32[]{:S(2)}) async-start(), calls=%async_computation | async-start | bytes 4456448 | tf_op jit(solution)/shard_map/all_gather | solution.py:354
  8.2 68.3 %collective-permute-start = (bf16[32,2,2048]{2,0,1:T(8,128)(2,1)S(1)}, bf16[32,2,2048]{2,0,1:T(8,128)(2,1)S(1)}, u32[]{:S(2)}, u32[]{:S(2)}) collective-permute-start(bf16[32,2,2048]{2,0,1:T(8,128)(2,1)S(1)} %fusion.33), channel_id=1, source_target_pairs={{0,16},{16,0},{1,17},{17,1},{2,18},{18,2},{3,19},{19,3},{4,20},{20... | collective-permute-start | bytes 786440 | tf_op jit(solution)/shard_map/ppermute | solution.py:339
  76.5 0.7 copy-start.5
  77.3 5.1 %copy-start.3 = (bf16[16,32,4096]{2,1,0:T(8,128)(2,1)S(1)}, bf16[16,32,4096]{2,1,0:T(8,128)(2,1)}, u32[]{:S(2)}) copy-start(bf16[16,32,4096]{2,1,0:T(8,128)(2,1)} %get-tuple-element.14) | copy-start | bytes 12582916
  77.3 12.6 %slice-start.2 = ((s8[6291456]{0:T(1024)(128)(4,1)}), s8[4194304]{0:T(1024)(128)(4,1)S(1)}, s32[]{:S(2)}) async-start(s8[6291456]{0:T(1024)(128)(4,1)} %bitcast.59), calls=%async_computation.3 | async-start | bytes 8388608
  77.3 16.5 %slice-start.4 = ((s8[6291456]{0:T(1024)(128)(4,1)}), s8[4194304]{0:T(1024)(128)(4,1)S(1)}, s32[]{:S(2)}) async-start(s8[6291456]{0:T(1024)(128)(4,1)} %bitcast.61), calls=%async_computation.5 | async-start | bytes 8388608
  82.4 7.5 %copy-start.4 = (bf16[16,32,4096]{2,1,0:T(8,128)(2,1)S(1)}, bf16[16,32,4096]{2,1,0:T(8,128)(2,1)}, u32[]{:S(2)}) copy-start(bf16[16,32,4096]{2,1,0:T(8,128)(2,1)} %get-tuple-element.15) | copy-start | bytes 12582916
  82.4 7.5 %slice-start.3 = ((s8[6291456]{0:T(1024)(128)(4,1)}), s8[2097152]{0:T(1024)(128)(4,1)S(1)}, s32[]{:S(2)}) async-start(s8[6291456]{0:T(1024)(128)(4,1)} %bitcast.59), calls=%async_computation.4 | async-start | bytes 4194304
  82.4 11.4 %slice-start.5 = ((s8[6291456]{0:T(1024)(128)(4,1)}), s8[2097152]{0:T(1024)(128)(4,1)S(1)}, s32[]{:S(2)}) async-start(s8[6291456]{0:T(1024)(128)(4,1)} %bitcast.61), calls=%async_computation.6 | async-start | bytes 4194304
  90.0 3.7 %copy-start.6 = (f32[16,32,128]{2,1,0:T(8,128)S(1)}, f32[16,32,128]{2,1,0:T(8,128)}, u32[]{:S(2)}) copy-start(f32[16,32,128]{2,1,0:T(8,128)} %get-tuple-element.16) | copy-start | bytes 786436
  93.6 8.1 %slice-start = ((s8[6291456]{0:T(1024)(128)(4,1)}), s8[2097152]{0:T(1024)(128)(4,1)S(1)}, s32[]{:S(2)}) async-start(s8[6291456]{0:T(1024)(128)(4,1)} %bitcast.57), calls=%async_computation.1 | async-start | bytes 4194304
  93.8 7.9 %slice-start.1 = ((s8[6291456]{0:T(1024)(128)(4,1)}), s8[4194304]{0:T(1024)(128)(4,1)S(1)}, s32[]{:S(2)}) async-start(s8[6291456]{0:T(1024)(128)(4,1)} %bitcast.57), calls=%async_computation.2 | async-start | bytes 8388608
  101.2 86.2 %collective-permute-start.1 = (bf16[512,2304]{1,0:T(8,128)(2,1)}, bf16[512,2304]{1,0:T(8,128)(2,1)}, u32[]{:S(2)}, u32[]{:S(2)}) collective-permute-start(bf16[512,2304]{1,0:T(8,128)(2,1)} %pad_maximum_fusion.4), channel_id=1, source_target_pairs={{0,16},{16,0},{1,17},{17,1},{2,18},{18,2},{3,19},{19,3},{4,20},{20... | collective-permute-start | bytes 7077896 | tf_op jit(solution)/shard_map/ppermute | solution.py:339
  123.2 63.6 %copy-start.7 = (s32[32,8]{0,1:T(8,128)S(1)}, s32[32,8]{0,1:T(8,128)}, u32[]{:S(2)}) copy-start(s32[32,8]{0,1:T(8,128)} %param.8) | copy-start | bytes 3076
  203.2 2.9 %copy-start.2 = (bf16[512,2048]{1,0:T(8,128)(2,1)S(1)}, bf16[512,2048]{1,0:T(8,128)(2,1)}, u32[]{:S(2)}) copy-start(bf16[512,2048]{1,0:T(8,128)(2,1)} %get-tuple-element.29) | copy-start | bytes 6291460
  203.2 4.2 %copy-start = (bf16[1024,2304]{1,0:T(8,128)(2,1)S(1)}, bf16[1024,2304]{1,0:T(8,128)(2,1)}, u32[]{:S(2)}) copy-start(bf16[1024,2304]{1,0:T(8,128)(2,1)} %pad_maximum_fusion) | copy-start | bytes 14155780
  212.5 5.0 %copy-start.1 = (bf16[512,2048]{1,0:T(8,128)(2,1)S(1)}, bf16[512,2048]{1,0:T(8,128)(2,1)}, u32[]{:S(2)}) copy-start(bf16[512,2048]{1,0:T(8,128)(2,1)} %get-tuple-element.28) | copy-start | bytes 6291460
Sparse Core Ops, SparseCore 0:
  77.4 54.1 all-gather.1

commit v3 on v2

--- a/solution.py
+++ b/solution.py
@@ -29,26 +29,27 @@
     return lax.axis_index("dp"), outer // lows, outer % lows, lax.axis_index("inner")
 
 
-def greet(sizes):
+def greet(sizes, groups):
     highs, lows, cores = sizes
     dp, hi, lo, core = place(sizes)
     peers = [(dp, (hi + d) % highs * lows + lo, core) for d in range(1, highs)]
     peers += [(dp, hi * lows + (lo + d) % lows, core) for d in range(1, lows)]
     peers += [(dp, hi * lows + lo, (core + d) % cores) for d in range(1, cores)]
+    peers += [((dp + d) % groups, hi * lows + lo, core) for d in range(1, groups)]
     barrier = pltpu.get_barrier_semaphore()
     for peer in peers:
         pl.semaphore_signal(barrier, inc=1, device_id=peer, device_id_type=MESH)
     pl.semaphore_wait(barrier, len(peers))
 
 
-def gather_kernel(sizes, chunks, *refs):
+def gather_kernel(sizes, groups, chunks, count, *refs):
     highs, lows, cores = sizes
-    count = len(refs) - 7
-    sources, results = refs[: count // 2], refs[count // 2 : count]
-    own_sem, hi_send, hi_recv, lo_send, lo_recv, core_send, core_recv = refs[count:]
+    sources, results = refs[:count], refs[count : 2 * count]
+    fars = refs[2 * count : -9]
+    own_sem, hi_send, hi_recv, lo_send, lo_recv, core_send, core_recv, far_send, far_recv = refs[-9:]
     dp, hi, lo, core = place(sizes)
     mine = (hi * lows + lo) * cores + core
-    greet(sizes)
+    greet(sizes, groups)
 
     def block_of(high, low, at_core):
         return (high * lows + low) * cores + at_core
@@ -100,12 +101,28 @@
             (core + e) % cores,
         )
 
+    def to_group(k, s):
+        src = sources[count - len(fars) + k]
+        share = src.shape[1] // groups
+        group = (dp + s) % groups
+        return pltpu.make_async_remote_copy(
+            src_ref=src.at[:, pl.ds(pl.multiple_of(group * share, share), share)],
+            dst_ref=fars[k].at[s - 1],
+            send_sem=far_send.at[k, s],
+            recv_sem=far_recv.at[k, s],
+            device_id=(group, hi * lows + lo, core),
+            device_id_type=MESH,
+        )
+
     sent = []
 
     def start(what):
         what.start()
         sent.append(what)
 
+    for k in range(len(fars)):
+        for s in range(1, groups):
+            start(to_group(k, s))
     for c in range(len(chunks)):
         for d in range(1, lows):
             start(to_lo(c, d, 0))
@@ -115,7 +132,7 @@
             start(to_core(c, 0, 0, e))
     kept = [
         pltpu.make_async_copy(sources[w], results[w].at[mine], own_sem.at[w])
-        for w in range(count // 2)
+        for w in range(count)
     ]
     for one in kept:
         one.start()
@@ -136,6 +153,9 @@
             for d in range(lows):
                 for e in range(1, cores):
                     to_core(c, d, h, e).wait_recv()
+    for k in range(len(fars)):
+        for s in range(1, groups):
+            to_group(k, s).wait_recv()
     for one in kept:
         one.wait()
     for one in sent:
@@ -156,17 +176,23 @@
     return chunks
 
 
-def gather_plane(arrays, width):
+def gather_plane(arrays, far_count, width):
+    groups = lax.axis_size("dp")
+    others = arrays[len(arrays) - far_count :] if groups > 1 else []
     sizes = highs, lows, cores = plane_sizes()
     blocks = highs * lows * cores
     chunks = cut(arrays, width)
     n = len(chunks)
     dma = pltpu.SemaphoreType.DMA
     got = pl.pallas_call(
-        functools.partial(gather_kernel, sizes, chunks),
-        out_shape=[jax.ShapeDtypeStruct((blocks,) + a.shape, a.dtype) for a in arrays],
+        functools.partial(gather_kernel, sizes, groups, chunks, len(arrays)),
+        out_shape=[jax.ShapeDtypeStruct((blocks,) + a.shape, a.dtype) for a in arrays]
+        + [
+            jax.ShapeDtypeStruct((groups - 1, a.shape[0], a.shape[1] // groups), a.dtype)
+            for a in others
+        ],
         in_specs=[pl.BlockSpec(memory_space=pl.ANY)] * len(arrays),
-        out_specs=[pl.BlockSpec(memory_space=pl.ANY)] * len(arrays),
+        out_specs=[pl.BlockSpec(memory_space=pl.ANY)] * (len(arrays) + len(others)),
         scratch_shapes=[
             dma((len(arrays),)),
             dma((n, highs)),
@@ -175,11 +201,14 @@
             dma((n, lows, highs)),
             dma((n, lows, highs, cores)),
             dma((n, lows, highs, cores)),
+            dma((far_count, groups)),
+            dma((far_count, groups)),
         ],
         compiler_params=pltpu.CompilerParams(collective_id=0, has_side_effects=True),
         cost_estimate=pl.CostEstimate(flops=0, bytes_accessed=150_000_000, transcendentals=0),
     )(*arrays)
-    return [g.reshape((-1,) + g.shape[2:]) for g in got]
+    whole = [g.reshape((-1,) + g.shape[2:]) for g in got[: len(arrays)]]
+    return whole, got[len(arrays) :]
 
 
 def scatter_kernel(sizes, chunks, count, *refs):
@@ -191,7 +220,7 @@
     )
     load_sem, core_send, core_recv, lo_send, lo_recv, hi_send, hi_recv = refs[2 * count + 5 * n :]
     dp, hi, lo, core = place(sizes)
-    greet(sizes)
+    greet(sizes, 1)
 
     def copy(src, dst, send, recv, outer, at_core):
         return pltpu.make_async_remote_copy(
@@ -357,12 +386,9 @@
     gate_grid = jnp.sum(jnp.where(chosen, gate_values[:, :, None], 0.0), axis=1)
 
     lanes = jnp.pad(gate_grid, ((0, 0), (0, -expert_count % 128)))
-    all_gates, all_tokens, all_upstream = gather_plane([lanes, tokens, upstream], 2048)
+    (all_gates, all_tokens, all_upstream), far = gather_plane([lanes, tokens, upstream], 2, 2048)
     all_gates = all_gates[:, :expert_count]
-    both = jnp.stack([tokens, upstream], axis=1)
-    far = exchange(lambda j: lax.dynamic_slice_in_dim(both, j * share, share, 2), groups)
-    *far, all_gates = lax.optimization_barrier((*far, all_gates))
-    far = [plane_gather(block) for block in far]
+    far = [[plane_gather(blocks[s]) for s in range(groups - 1)] for blocks in far]
 
     is_mine = jnp.arange(expert_count, dtype=jnp.int32) == expert
     gate = jnp.sum(jnp.where(is_mine[None, :], all_gates, 0.0), axis=1, keepdims=True)
@@ -393,20 +419,19 @@
     grad_gates = jnp.sum(jnp.where(chosen, dots[:, None, :expert_count], 0.0), axis=2)
 
     ff = gate_mat.shape[1]
-    rows = jnp.concatenate(
-        [lax.dynamic_slice_in_dim(all_tokens, me * share, share, 1)]
-        + [block[:, 0] for block in far],
-        axis=0,
-    )
-    ups = jnp.concatenate(
-        [lax.dynamic_slice_in_dim(all_upstream, me * share, share, 1)]
-        + [block[:, 1] for block in far],
-        axis=0,
-    )
-    every = jnp.concatenate([packed] + far_packed, axis=0)
-    grad_w_gate = dot(rows, every[:, :ff], 0, 0).astype(jnp.bfloat16)[None]
-    grad_w_up = dot(rows, every[:, ff : 2 * ff], 0, 0).astype(jnp.bfloat16)[None]
-    grad_w_down = dot(every[:, 2 * ff :], ups, 0, 0).astype(jnp.bfloat16)[None]
+    rows = [lax.dynamic_slice_in_dim(all_tokens, me * share, share, 1), *far[0]]
+    ups = [lax.dynamic_slice_in_dim(all_upstream, me * share, share, 1), *far[1]]
+    every = [packed, *far_packed]
+
+    def summed(lefts, rights):
+        total = dot(lefts[0], rights[0], 0, 0)
+        for left, right in zip(lefts[1:], rights[1:]):
+            total += dot(left, right, 0, 0)
+        return total.astype(jnp.bfloat16)[None]
+
+    grad_w_gate = summed(rows, [each[:, :ff] for each in every])
+    grad_w_up = summed(rows, [each[:, ff : 2 * ff] for each in every])
+    grad_w_down = summed([each[:, 2 * ff :] for each in every], ups)
     return (output, grad_tokens, grad_gates, grad_w_gate, grad_w_up, grad_w_down)
 
 

time: 231 us -> 237 us (1.026)
  matrix products: 53.1 us -> 74.9 us
  other arithmetic: 20 us -> 4.27 us
  Pallas kernels: 127 us -> 139 us
  local copies, waits for them, and re-layouts: 12.3 us -> 2.92 us
    dot_general x9 -> x12, matrix products: 53.1 us -> 74.9 us  [dot(): lax.dot_general(left, right, (((left_dim,), (right_dim,)), ((), ())), pre...]
    concatenate x1 -> x0, other arithmetic: 15.8 us -> none  [local(): every = jnp.concatenate([packed] + far_packed, axis=0)]
    pallas_call x1, Pallas kernels: 63.5 us -> 73.2 us  [scatter_plane(): pl.pallas_call(functools.partial(scatter_kernel, sizes, chunks, len(array...]
    dynamic_slice x1 -> x0, local copies, waits for them, and re-layouts: 5.1 us -> none  [local(): lax.dynamic_slice_in_dim(all_upstream, me * share, share, 1)]
    squeeze x1 -> x0, local copies, waits for them, and re-layouts: 2.69 us -> none  [local(): block[:, 1]]
  transfers between devices with their start and end apart: 3 -> 3, of which waited for: 0 -> 0; matrix products, arithmetic and copies ran while one was open for 27% -> 30% of each run, Pallas kernels for 55% -> 31%
where the time goes in v3:
time: 237 us
  Pallas kernels  139 us (59%)
  matrix products  74.9 us (32%)
  between operations  14.2 us (6%)
  other arithmetic  4.27 us (2%)
  local copies, waits for them, and re-layouts  2.92 us (1%)
    dot_general x12, matrix products, dot(): lax.dot_general(left, right, (((left_dim,), (right_dim,)), ((), ())), pre...  74.9 us
    pallas_call x1, Pallas kernels, scatter_plane(): pl.pallas_call(functools.partial(scatter_kernel, sizes, chunks, len(array...  73.2 us
    pallas_call x1, Pallas kernels, gather_plane(): pl.pallas_call(functools.partial(gather_kernel, sizes, groups, chunks, le...  65.5 us
  transfers between devices with their start and end apart: 3, of which 0 were waited for; matrix products, arithmetic and copies ran while one was open for 30% of the time, Pallas kernels for 31%

profile of v3, /device:TPU:0, one launch (start us, length us, event | category | flops | bytes accessed | tf_op | source)
XLA Modules:
  0.0 237.1 jit_solution(13392152350929967461)
XLA Ops:
  7.2 0.7 select_reduce_fusion.1
  8.0 0.6 pad.4.refs_0_
  8.6 65.5 %shard_map.118 = (f32[16,32,128]{2,1,0:T(8,128)}, bf16[16,32,4096]{2,1,0:T(8,128)(2,1)}, bf16[16,32,4096]{2,1,0:T(8,128)(2,1)}, bf16[1,32,2048]{2,1,0:T(8,128)(2,1)}, bf16[1,32,2048]{2,1,0:T(8,128)(2,1)}) custom-call(f32[32,128]{1,0:T(8,128)} %pad.4.refs_0_, bf16[32,4096]{1,0:T(8,128)(2,1)} %refs_1_.1, bf16[32,4096]{1,0:T(8,128)(2,1)} %refs_2_.1), custom_call_target="tpu_custom_call" | custom-call | bytes 150000000 | tf_op jit(solution)/shard_map/pallas_call | solution.py:187
  74.2 1.2 fusion.33
  75.5 7.2 %fusion.6 = f32[512,768]{1,0:T(8,128)S(1)} fusion(bf16[512,4096]{1,0:T(8,128)(2,1)} %bitcast.58, bf16[1,4096,768]{2,1,0:T(8,128)(2,1)} %param.12), kind=kOutput, calls=%fused_computation.7 | convolution fusion | flops 3221225472 | bytes 12058624 | tf_op jit(solution)/shard_map/dot_general | solution.py:14
  82.7 3.5 %fusion.2 = f32[512,768]{1,0:T(8,128)S(1)} fusion(bf16[512,4096]{1,0:T(8,128)(2,1)S(1)} %bitcast.54, bf16[1,768,4096]{2,1,0:T(8,128)(2,1)S(1)} %bitcast.57), kind=kOutput, calls=%fused_computation.3 | convolution fusion | flops 3221225472 | bytes 12058624 | tf_op jit(solution)/shard_map/dot_general | solution.py:14
  86.2 0.6 copy-done.4
  86.8 4.3 %multiply_convert_fusion.1 = (bf16[512,768]{1,0:T(8,128)(2,1)S(1)}, f32[512]{0:T(512)S(1)}, bf16[512,768]{1,0:T(8,128)(2,1)S(1)}, bf16[512,768]{1,0:T(8,128)(2,1)S(1)}) fusion(f32[512,768]{1,0:T(8,128)S(1)} %fusion.6, f32[512,768]{1,0:T(8,128)S(1)} %fusion.2, f32[512]{0:T(512)S(1)} %fusion.33, bf16[512,4096]{1,0:T(8,128)(2,1)S(1)} %bitcast.59, ...), kind=kOutput, calls=%fused_computation.31 | convolution fusion | flops 3228696064 | bytes 15994880 | tf_op jit(solution)/shard_map/dot_general | solution.py:14
  91.1 1.6 pad_maximum_fusion
  92.7 2.0 collective-permute-start
  94.7 8.4 %fusion.4 = f32[512,4096]{1,0:T(8,128)} fusion(bf16[512,768]{1,0:T(8,128)(2,1)S(1)} %get-tuple-element.24, bf16[1,4096,768]{2,1,0:T(8,128)(2,1)} %param.12), kind=kOutput, calls=%fused_computation.5 | convolution fusion | flops 3221225472 | bytes 15466496 | tf_op jit(solution)/shard_map/dot_general | solution.py:14
  103.2 7.7 %fusion.12 = bf16[512,4096]{1,0:T(8,128)(2,1)} fusion(bf16[512,768]{1,0:T(8,128)(2,1)S(1)} %get-tuple-element.25, bf16[1,768,4096]{2,1,0:T(8,128)(2,1)} %param.13), kind=kOutput, calls=%fused_computation.16 | convolution fusion | flops 3223322624 | bytes 11272192 | tf_op jit(solution)/shard_map/dot_general | solution.py:14
  111.0 0.1 broadcast_select_fusion.refs_0_
  111.1 9.3 %add_convert_fusion = bf16[512,4096]{1,0:T(8,128)(2,1)} fusion(f32[512,4096]{1,0:T(8,128)} %fusion.4, bf16[512,768]{1,0:T(8,128)(2,1)S(1)} %get-tuple-element.22, bf16[1,4096,768]{2,1,0:T(8,128)(2,1)} %param.11), kind=kOutput, calls=%fused_computation | convolution fusion | flops 3225419776 | bytes 19660800 | tf_op jit(solution)/shard_map/dot_general | solution.py:14
  120.4 73.2 %shard_map.119 = (f32[32,128]{1,0:T(8,128)S(1)}, bf16[32,4096]{1,0:T(8,128)(2,1)S(1)}, bf16[32,4096]{1,0:T(8,128)(2,1)S(1)}) custom-call(f32[4,2,2,32,128]{4,3,2,1,0:T(8,128)S(1)} %broadcast_select_fusion.refs_0_, bf16[4,2,2,32,4096]{4,3,2,1,0:T(8,128)(2,1)S(1)} %bitcast.50, bf16[4,2,2,32,4096]{4,3,2,1,0:T(8,128)(2,1)} %bitcast.52), custom_call_target="tpu_custom_call" | custom-call | bytes 180000000 | tf_op jit(solution)/shard_map/pallas_call | solution.py:337
  193.7 0.6 select_reduce_fusion
  194.3 6.2 %fusion.23 = f32[768,2048]{1,0:T(8,128)} fusion(bf16[512,768]{1,0:T(8,128)(2,1)S(1)} %get-tuple-element.25, bf16[512,4096]{1,0:T(8,128)(2,1)} %bitcast.53, s32[]{:T(128)S(6)} %select_n.25), kind=kOutput, calls=%fused_computation.24 | convolution fusion | flops 1610612736 | bytes 9175044 | tf_op jit(solution)/shard_map/dot_general | solution.py:14
  200.6 4.5 %fusion.25 = f32[2048,768]{1,0:T(8,128)} fusion(bf16[512,768]{1,0:T(8,128)(2,1)S(1)} %get-tuple-element.24, bf16[512,4096]{1,0:T(8,128)(2,1)S(1)} %bitcast.60, s32[]{:T(128)S(6)} %select_n.25), kind=kOutput, calls=%fused_computation.26 | convolution fusion | flops 1610612736 | bytes 9175044 | tf_op jit(solution)/shard_map/dot_general | solution.py:14
  205.0 4.5 %fusion.27 = f32[2048,768]{1,0:T(8,128)} fusion(bf16[512,768]{1,0:T(8,128)(2,1)S(1)} %get-tuple-element.22, bf16[512,4096]{1,0:T(8,128)(2,1)S(1)} %bitcast.61, s32[]{:T(128)S(6)} %select_n.25), kind=kOutput, calls=%fused_computation.28 | convolution fusion | flops 1610612736 | bytes 9175044 | tf_op jit(solution)/shard_map/dot_general | solution.py:14
  209.6 7.3 %fusion.18 = bf16[1,2048,768]{2,1,0:T(8,128)(2,1)} fusion(f32[2048,768]{1,0:T(8,128)} %fusion.25, bf16[1,512,2048]{2,1,0:T(8,128)(2,1)} %all-gather.5.cloned.1.call-done, bf16[512,2304]{1,0:T(8,128)(2,1)} %collective-permute-done), kind=kOutput, calls=%fused_computation.18 | convolution fusion | flops 1613758464 | bytes 12320768 | tf_op jit(solution)/shard_map/dot_general | solution.py:14
  216.9 4.8 %fusion.17 = bf16[1,2048,768]{2,1,0:T(8,128)(2,1)} fusion(f32[2048,768]{1,0:T(8,128)S(1)} %copy-done.7, bf16[1,512,2048]{2,1,0:T(8,128)(2,1)S(1)} %copy-done.6, bf16[512,2304]{1,0:T(8,128)(2,1)} %collective-permute-done), kind=kOutput, calls=%fused_computation.17 | convolution fusion | flops 1613758464 | bytes 12320768 | tf_op jit(solution)/shard_map/dot_general | solution.py:14
  221.7 7.2 %fusion.19 = bf16[1,768,2048]{2,1,0:T(8,128)(2,1)} fusion(f32[768,2048]{1,0:T(8,128)} %fusion.23, bf16[1,512,2048]{2,1,0:T(8,128)(2,1)} %all-gather.7.cloned.1.call-done, bf16[512,2304]{1,0:T(8,128)(2,1)} %collective-permute-done), kind=kOutput, calls=%fused_computation.19 | convolution fusion | flops 1613758464 | bytes 12320768 | tf_op jit(solution)/shard_map/dot_general | solution.py:14
  228.9 0.7 copy.19
  229.6 0.7 copy.20
  (32 shorter events, 0.4 us)
Async XLA Ops:
  7.2 202.4 %all-gather.5.cloned.1.call-start = ((), (), s32[]{:S(2)}) async-start(), calls=%async_computation | async-start | bytes 2228224 | tf_op jit(solution)/shard_map/all_gather | solution.py:383
  74.1 8.5 %slice-start = ((s8[6291456]{0:T(1024)(128)(4,1)}), s8[2097152]{0:T(1024)(128)(4,1)S(1)}, s32[]{:S(2)}) async-start(s8[6291456]{0:T(1024)(128)(4,1)} %bitcast.56), calls=%async_computation.2 | async-start | bytes 4194304
  74.2 147.6 %all-gather.7.cloned.1.call-start = ((), (), s32[]{:S(2)}) async-start(), calls=%async_computation.1 | async-start | bytes 2228224 | tf_op jit(solution)/shard_map/all_gather | solution.py:383
  75.5 7.2 %copy-start.1 = (bf16[16,32,4096]{2,1,0:T(8,128)(2,1)S(1)}, bf16[16,32,4096]{2,1,0:T(8,128)(2,1)}, u32[]{:S(2)}) copy-start(bf16[16,32,4096]{2,1,0:T(8,128)(2,1)} %get-tuple-element.15) | copy-start | bytes 12582916
  75.5 7.2 %slice-start.1 = ((s8[6291456]{0:T(1024)(128)(4,1)}), s8[4194304]{0:T(1024)(128)(4,1)S(1)}, s32[]{:S(2)}) async-start(s8[6291456]{0:T(1024)(128)(4,1)} %bitcast.56), calls=%async_computation.3 | async-start | bytes 8388608
  82.7 3.5 %copy-start.3 = (bf16[1,4096,768]{2,1,0:T(8,128)(2,1)S(1)}, bf16[1,4096,768]{2,1,0:T(8,128)(2,1)}, u32[]{:S(2)}) copy-start(bf16[1,4096,768]{2,1,0:T(8,128)(2,1)} %param.11) | copy-start | bytes 18874372
  82.7 4.1 %copy-start.4 = (bf16[16,32,4096]{2,1,0:T(8,128)(2,1)S(1)}, bf16[16,32,4096]{2,1,0:T(8,128)(2,1)}, u32[]{:S(2)}) copy-start(bf16[16,32,4096]{2,1,0:T(8,128)(2,1)} %get-tuple-element.14) | copy-start | bytes 12582916
  92.7 116.9 %collective-permute-start = (bf16[512,2304]{1,0:T(8,128)(2,1)}, bf16[512,2304]{1,0:T(8,128)(2,1)}, u32[]{:S(2)}, u32[]{:S(2)}) collective-permute-start(bf16[512,2304]{1,0:T(8,128)(2,1)} %pad_maximum_fusion), channel_id=1, source_target_pairs={{0,16},{16,0},{1,17},{17,1},{2,18},{18,2},{3,19},{19,3},{4,20},{20... | collective-permute-start | bytes 7077896 | tf_op jit(solution)/shard_map/ppermute | solution.py:368
  111.1 9.3 %copy-start = (bf16[512,4096]{1,0:T(8,128)(2,1)S(1)}, bf16[512,4096]{1,0:T(8,128)(2,1)}, u32[]{:S(2)}) copy-start(bf16[512,4096]{1,0:T(8,128)(2,1)} %fusion.12) | copy-start | bytes 12582916
  120.4 73.3 %copy-start.2 = (s32[32,8]{0,1:T(8,128)S(1)}, s32[32,8]{0,1:T(8,128)}, u32[]{:S(2)}) copy-start(s32[32,8]{0,1:T(8,128)} %param.8) | copy-start | bytes 3076
  194.3 6.2 %copy-start.5 = (bf16[16,32,4096]{2,1,0:T(8,128)(2,1)S(1)}, bf16[16,32,4096]{2,1,0:T(8,128)(2,1)}, u32[]{:S(2)}) copy-start(bf16[16,32,4096]{2,1,0:T(8,128)(2,1)} %get-tuple-element.14) | copy-start | bytes 12582916
  209.6 7.3 %copy-start.6 = (bf16[1,512,2048]{2,1,0:T(8,128)(2,1)S(1)}, bf16[1,512,2048]{2,1,0:T(8,128)(2,1)}, u32[]{:S(2)}) copy-start(bf16[1,512,2048]{2,1,0:T(8,128)(2,1)} %all-gather.5.cloned.1.call-done) | copy-start | bytes 6291460
  209.6 7.3 %copy-start.7 = (f32[2048,768]{1,0:T(8,128)S(1)}, f32[2048,768]{1,0:T(8,128)}, u32[]{:S(2)}) copy-start(f32[2048,768]{1,0:T(8,128)} %fusion.27) | copy-start | bytes 18874372
Sparse Core Ops, SparseCore 0:
  74.3 45.0 all-gather.4
  121.5 54.2 all-gather.6
